TPU v7x, 32 devices: a whole 2x2x4 slice. The times are simulated.
32 devices in a mesh: grp: 2 (over x), gx: 16 (over z, y, core).
Axes of the slice: x: 2, y: 2, z: 4, core: 2. Of those that a mesh axis runs over, the one named last changes fastest.
Arguments:
- rhs: float32 [640, 12800], P(('grp', 'gx')), parts along dimension 0, may hold values from -4 to 4
- accumulation: bfloat16 [640, 12800], P(('grp', 'gx')), parts along dimension 0, may hold values from 0.0099487305 to 0.099609375
- trans_x: bfloat16 [640, 12800], P(('grp', 'gx')), parts along dimension 0, may hold values from 0.049804688 to 1
- trans_y: bfloat16 [640, 12800], P(('grp', 'gx')), parts along dimension 0, may hold values from 0.049804688 to 1
- trans_z: bfloat16 [640, 12800], P(('grp', 'gx')), parts along dimension 0, may hold values from 0.049804688 to 1
- basis_center: bfloat16 [640, 12800], P(('grp', 'gx')), parts along dimension 0, may hold values from 0.5 to 1
- basis_side: bfloat16 [2, 640, 12800], P(None, ('grp', 'gx')), parts along dimension 1, may hold values from 0 to 0.5
- coarse_inverse: float32 [64, 128], P(('grp', 'gx')), parts along dimension 0, may hold values from 0.001 to 0.004
Outputs:
- correction: float32 [640, 12800], P(('grp', 'gx')), parts along dimension 0
- coarse_update: float32 [64, 128], P(('grp', 'gx')), parts along dimension 0
There are 2 independent parts, one for each index of `grp`. A program takes and returns all parts, laid end to end along the dimension named above; each array names one. Nothing has to cross between parts.
All inputs are finite; a program needn't handle non-finite values.
Results may differ from a plain program's by a relative error of at most 0.0003.
Values may be sent and summed in bfloat16 or wider, within the bound.
No kernel may reach another device: no remote copies, remote signals or barrier semaphores. Data moves between devices by JAX's collectives and lax.ppermute only.
A program may use at most 64 MiB of HBM per device.

v0:
```python
import jax
import jax.numpy as jnp
from jax import lax
from jax.experimental import pallas as pl
from jax.experimental.pallas import tpu as pltpu
from jax.sharding import PartitionSpec as P

BLK = 10
NCY = 8
NCZ = 16
CSW = 6
NZ = 160
PLANE = 12800
COARSE = NCY * NCZ
OMEGA_FINE = 0.7
OMEGA_COARSE = 0.6

LANES = 128
TILES = PLANE // LANES
PHASES = 5
PAIR = 25
PAIRS = TILES // PAIR
OWN = 20
TOP = 8
PAD = 32
GROUP = 20
QUARTERS = 4
LT = QUARTERS * NZ // LANES
PAIRED = ((0, 0), (0, 1), (0, 2), (1, 1), (1, 2), (2, 2))
PLANES = 16
WHOLE = TILES // 16
REST = TILES % 16
OFFSET = (0, -1, 1)
SAME = ((0, 0), (0, 1), (0, 2), (0, 3), (1, 1), (1, 2), (1, 3), (2, 2), (2, 3), (3, 3), (1, 4), (2, 4), (3, 4))
ACROSS = tuple((u, v) for u in range(4) for v in range(4) if abs(u - v) <= 2)
Y_ROW = len(SAME)
Z_ROW = Y_ROW + len(ACROSS)
INVERSE_ROW = Z_ROW + len(ACROSS)
RHS_ROW = INVERSE_ROW + 2
ALL_ROWS = 48
F32 = jnp.float32
BF16 = jnp.bfloat16


def params(mib):
    return pltpu.CompilerParams(vmem_limit_bytes=mib << 20)


def vmem(shape, dtype=F32):
    return pltpu.VMEM(shape, dtype)


def in_vmem(count):
    return [pl.BlockSpec(memory_space=pltpu.VMEM)] * count


def in_hbm(count):
    return [pl.BlockSpec(memory_space=pltpu.HBM)] * count


def padded():
    return vmem((TILES * PAD, LANES))


def padded_out():
    return pltpu.HBM((TILES * PAD, LANES), F32)


def cells(dtype=BF16):
    return vmem((OWN, PLANE), dtype)


def semaphores(*shape):
    return pltpu.SemaphoreType.DMA(shape)


def stream(sources, buffers, sems):
    width = PLANE // PAIRS

    def copy(field, n):
        lanes = pl.ds(pl.multiple_of(n * width, width), width)
        return pltpu.make_async_copy(
            sources[field].at[:, lanes], buffers[field].at[:, lanes], sems.at[field, n]
        )

    for n in range(PAIRS):
        for field in range(len(sources)):
            copy(field, n).start()

    def wait(n):
        for field in range(len(sources)):
            copy(field, n).wait()

    return wait


def copies(sources, targets, sems):
    made = [
        pltpu.make_async_copy(src, dst, sems.at[n])
        for n, (src, dst) in enumerate(zip(sources, targets))
    ]
    for copy in made:
        copy.start()
    return made


def lane_roll(value, steps):
    return pltpu.roll(value, steps % LANES, 1)


def lanes_of(rows):
    return lax.broadcasted_iota(jnp.int32, (rows, LANES), 1)


def rows_of(rows):
    return lax.broadcasted_iota(jnp.int32, (rows, LANES), 0)


def at(t):
    return pl.ds(pl.multiple_of(t * LANES, LANES), LANES)


def span(t, low, count):
    return pl.ds(t * PAD + low, count)


def own(ref, t):
    return ref[:, at(t)].astype(F32)


def over_tiles(body, carry, before=None, unroll=1):
    def step(n, carry):
        if before is not None:
            before(n)
        for i in range(PAIR):
            carry = body(n * PAIR + i, i, carry)
        return carry

    return lax.fori_loop(0, PAIRS, step, carry, unroll=unroll)


def halves(value):
    high = value.astype(BF16)
    low = (value - high.astype(F32)).astype(BF16)
    return high, low


def remainder(value):
    return value - value.astype(BF16).astype(F32)


def parity():
    return lax.rem(lax.axis_index("gx"), 2)


def coupled(src, tx, ty, tz, t, low, count, carry):
    center, following, y_next, z_flux, y_flux, y_flux_before = carry
    lane = lanes_of(count)
    here = span(t, low, count)
    second = src[span(jnp.minimum(t + 2, TILES - 1), low, count), :]
    z_up = jnp.where(lane == LANES - 1, lane_roll(following, -1), lane_roll(center, -1))
    y_second = lane_roll(second, -(NZ - LANES))
    y_up = jnp.where(lane >= 2 * LANES - NZ, y_second, y_next)
    tz_t = tz[here, :]
    ty_t = ty[here, :]
    z_flux_new = lane_roll(tz_t * center, 1)
    z_down = jnp.where(lane == 0, z_flux, z_flux_new)
    y_down = jnp.where(lane < NZ - LANES, y_flux_before, y_flux)
    y_flux_new = lane_roll(ty_t * center, NZ - LANES)
    total = tz_t * z_up + z_down
    total = total + (ty_t * y_up + y_down)
    total = total + tx[here, :] * src[span(t, low + 1, count), :]
    total = total + tx[span(t, low - 1, count), :] * src[span(t, low - 1, count), :]
    return total, (following, second, y_second, z_flux_new, y_flux_new, y_flux)


def coupled_start(src, low, count):
    center = src[span(0, low, count), :]
    following = src[span(1, low, count), :]
    zero = center * 0.0
    return center, following, lane_roll(following, -(NZ - LANES)), zero, zero, zero


def sweep(src, dst, tx, ty, tz, k, b, low, count):
    def body(t, i, carry):
        total, after = coupled(src, tx, ty, tz, t, low, count, carry)
        here = span(t, low, count)
        dst[here, :] = b[here, :] + (1.0 - OMEGA_FINE) * carry[0] + k[here, :] * total
        return after

    over_tiles(body, coupled_start(src, low, count), unroll=2)


def plane(ref, row, q, size, stride=PAD):
    return pl.ds(16 * q * stride + row, size, stride)


def read_plane(ref, row, stride=PAD):
    return lambda q, size: ref[plane(ref, row, q, size, stride), :]


def send_both(pay_a, pay_b, tail_a, tail_b, right, left):
    even = parity() == 0
    for n in range(PLANES):
        for q in range(WHOLE + 1):
            size = 16 if q < WHOLE else REST
            r, l = right[n](q, size), left[n](q, size)
            a, b = jnp.where(even, r, l), jnp.where(even, l, r)
            if q < WHOLE:
                rows = slice((n * WHOLE + q) * 16, (n * WHOLE + q) * 16 + 16)
                pay_a[rows, :] = a.astype(BF16)
                pay_b[rows, :] = b.astype(BF16)
            else:
                rows = slice(n * REST, n * REST + REST)
                tail_a[rows, :] = a
                tail_b[rows, :] = b
    pay_a[PLANES * WHOLE * 16 :, :] = tail_a[...].astype(BF16)
    pay_b[PLANES * WHOLE * 16 :, :] = tail_b[...].astype(BF16)


def received(got_a, got_b, tail_a, tail_b):
    even = parity() == 0
    tail_a[...] = got_a[PLANES * WHOLE * 16 :, :].astype(F32)
    tail_b[...] = got_b[PLANES * WHOLE * 16 :, :].astype(F32)

    def both(n, q):
        if q < WHOLE:
            rows = slice((n * WHOLE + q) * 16, (n * WHOLE + q) * 16 + 16)
            a, b = got_a[rows, :].astype(F32), got_b[rows, :].astype(F32)
        else:
            rows = slice(n * REST, n * REST + REST)
            a, b = tail_a[rows, :], tail_b[rows, :]
        return jnp.where(even, b, a), jnp.where(even, a, b)

    return both


def payload():
    return jax.ShapeDtypeStruct((PLANES * TILES, LANES), BF16)


def tails():
    return [vmem((PLANES * REST, LANES))] * 2


def prepare_kernel(
    rhs, accum, trans_x, trans_y, trans_z, center, first_side, pay_a, pay_b,
    rhs_v, accum_v, x_v, y_v, z_v, center_v, raw, tx, ty, tz, dg, basis, tail_a, tail_b, sems,
):
    wait = stream(
        (rhs, accum, trans_x, trans_y, trans_z, center.at[0:16, :]),
        (rhs_v, accum_v, x_v, y_v, z_v, center_v),
        sems,
    )
    lane = lanes_of(12)

    def ends(ref, t):
        value = own(ref, t)
        return jnp.concatenate([value[0:8], value[16:20]], axis=0)

    def body(t, i, carry):
        z_before, y_before, y_second = carry
        z_pos = (i * LANES + lane) % NZ
        cells = t * LANES + lane
        here = pl.ds(t * 24 + 8, 12)
        x, y, z = ends(x_v, t), ends(y_v, t), ends(z_v, t)
        y_inner = jnp.where(cells < PLANE - NZ, y, 0.0)
        z_inner = jnp.where(z_pos != NZ - 1, z, 0.0)
        z_rolled = lane_roll(z_inner, 1)
        y_rolled = lane_roll(y_inner, NZ - LANES)
        tx[pl.ds(t * 24, 8), :] = jnp.zeros((8, LANES), F32)
        tx[here, :] = x
        ty[here, :] = y_inner
        tz[here, :] = z_inner
        total = ends(accum_v, t) + x + tx[pl.ds(t * 24 + 7, 12), :]
        total = total + y + jnp.where(lane < NZ - LANES, y_second, y_before)
        total = total + z + jnp.where(lane == 0, z_before, z_rolled)
        dg[here, :] = total
        raw[here, :] = ends(rhs_v, t)
        basis[pl.ds(t * 8, 2), :] = first_side[:, at(t)].astype(F32)
        basis[pl.ds(t * 8 + 2, 1), :] = center_v[:, at(t)].astype(F32)[0:1]
        return z_rolled, y_rolled, y_before

    zero = lanes_of(12).astype(F32) * 0.0
    over_tiles(body, (zero, zero, zero), wait)

    def low_part(f):
        return lambda q, size: remainder(f(q, size))

    def first_sweep(row):
        r, d = read_plane(raw, row, 24), read_plane(dg, row, 24)
        return lambda q, size: OMEGA_FINE * r(q, size) / d(q, size)

    def planes(near, second, far, x_rows):
        r, d = read_plane(raw, near, 24), read_plane(dg, near, 24)
        return (
            [r, low_part(r), read_plane(raw, second, 24)]
            + [d, low_part(d), read_plane(dg, second, 24)]
            + [read_plane(ref, row, 24) for ref in (ty, tz) for row in (near, second)]
            + [first_sweep(far)]
            + [read_plane(tx, row, 24) for row in x_rows]
        )

    right = planes(19, 18, 17, (19, 18, 17))
    left = planes(8, 9, 10, (8, 9))
    weights = [read_plane(basis, row, 8) for row in (2, 0, 1)]
    send_both(pay_a, pay_b, tail_a, tail_b, right + weights[:2], left + weights)


def prepare(rhs, accum, trans_x, trans_y, trans_z, center, first_side):
    return pl.pallas_call(
        prepare_kernel,
        out_shape=(payload(),) * 2,
        in_specs=in_hbm(6) + in_vmem(1),
        out_specs=tuple(in_vmem(2)),
        scratch_shapes=[cells(F32)]
        + [cells()] * 4
        + [vmem((16, PLANE), BF16)]
        + [vmem((TILES * 24, LANES))] * 5
        + [vmem((TILES * 8, LANES))]
        + tails()
        + [semaphores(6, PAIRS)],
        compiler_params=params(58),
    )(rhs, accum, trans_x, trans_y, trans_z, center, first_side)


def add_share(shares, u, v, value):
    pair = (min(u, v), max(u, v))
    shares[pair] = shares[pair] + value if pair in shares else value


def add_face(shares, u, v, value):
    add_share(shares, u, v, -2.0 * value if u == v else -value)


def presmooth_kernel(
    got_a, got_b, raw, tx_in, ty_in, tz_in, dg_in, w0, w1, w2, operator,
    tx, ty, tz, dg, tx_out, ty_out, tz_out, k_out, b_out, smooth_out, w0_out, w1_out, w2_out,
    part, pay_a, pay_b,
    k, b, smooth, work, sums, rest, edges, tail_a, tail_b, out_sems,
):
    weights = (w0, w1, w2)
    sent = copies(weights, (w0_out, w1_out, w2_out), out_sems.at[0:3])
    both = received(got_a, got_b, tail_a, tail_b)
    for q in range(WHOLE + 1):
        size = 16 if q < WHOLE else REST

        def put(ref, row, value):
            ref[plane(ref, row, q, size), :] = value

        def get(ref, row):
            return ref[plane(ref, row, q, size), :]

        values = [both(n, q) for n in range(PLANES)]
        left, right = [v[0] for v in values], [v[1] for v in values]
        for got, rows in ((left, (7, 6, 5)), (right, (28, 29, 30))):
            put(b, rows[0], got[0] + got[1])
            put(b, rows[1], got[2])
            put(dg, rows[1], got[5])
            put(ty, rows[0], got[6])
            put(ty, rows[1], got[7])
            put(tz, rows[0], got[8])
            put(tz, rows[1], got[9])
            put(b, rows[2], got[10])
            put(tx, rows[0], got[11])
            put(tx, rows[1], got[12])
        put(tx, 5, left[13])
        tx_before = left[11]
        tx_last = get(tx, TOP + OWN - 1)
        beyond = right[3] + right[4]
        put(dg, 7, left[3] + left[4])
        put(dg, 28, jnp.where(beyond > 0.0, beyond + tx_last, 0.0))
        put(dg, TOP, get(dg, TOP) + tx_before)
        first = [get(w, TOP) for w in weights]
        last = [get(w, TOP + OWN - 1) for w in weights]
        from_next = [right[13], right[14], right[15]]
        products = [tx_last * last[a] * from_next[c] for a in range(3) for c in range(3)]
        products += [tx_before * first[a] * first[c] for a, c in PAIRED]
        for n, value in enumerate(products):
            edges[plane(edges, n, q, size, 16), :] = value
        edges[plane(edges, 15, q, size, 16), :] = tx_last * 0.0

    sent += copies((tx, ty, tz), (tx_out, ty_out, tz_out), out_sems.at[3:6])

    def scale(t, i, carry):
        here = span(t, 6, 24)
        diag = dg[here, :]
        value = jnp.where(diag > 0.0, OMEGA_FINE / diag, 0.0)
        k[here, :] = value
        b[span(t, TOP, OWN), :] = raw[span(t, TOP, OWN), :]
        b[here, :] = value * b[here, :]
        return carry

    over_tiles(scale, 0)
    sent += copies((k, b), (k_out, b_out), out_sems.at[6:8])
    sweep(b, work, tx, ty, tz, k, b, 6, 24)
    sweep(work, smooth, tx, ty, tz, k, b, 7, 22)
    sent += copies((smooth,), (smooth_out,), out_sems.at[8:9])
    planes_r, planes_l = [], []
    for planes, rows in ((planes_r, (19, 18, 17)), (planes_l, (0, 1, 2))):
        for row in rows:
            f = read_plane(smooth, TOP + row)
            planes += [f, (lambda f: lambda q, size: remainder(f(q, size)))(f)]
        planes += [read_plane(w, TOP + row) for w in weights for row in rows]
        planes += [planes[-1]]
    send_both(pay_a, pay_b, tail_a, tail_b, planes_r, planes_l)

    sums[...] = jnp.zeros_like(sums)
    lane = lanes_of(64)
    row8 = rows_of(8)
    for n in range(PAIR):
        rest[n * 24 + 16 : n * 24 + 24, :] = jnp.zeros((8, LANES), F32)

    def residual(t, i, carry):
        total, following = coupled(smooth, tx, ty, tz, t, TOP, OWN, carry)
        rest[i * 24 : i * 24 + OWN, :] = (
            raw[span(t, TOP, OWN), :] - dg[span(t, TOP, OWN), :] * carry[0] + total
        )
        left_over = rest[i * 24 : i * 24 + 24, :]
        folded = []
        for w in weights:
            f = w[span(t, TOP, 24), :] * left_over
            mixed = jnp.where(row8 < BLK - 8, f[8:16], 0.0)
            folded += [f[0:8] + mixed, f[16:24] + (f[8:16] - mixed)]
        folded = jnp.concatenate(folded + [edges[pl.ds(t * 16, 16), :]], axis=0)
        n = t // PAIR
        phase = i % PHASES
        if i != PAIR // 2:
            sums[phase, 2 * n + (1 if i > PAIR // 2 else 0)] += folded
        else:
            sums[phase, 2 * n] += jnp.where(lane < LANES // 2, folded, 0.0)
            sums[phase, 2 * n + 1] += jnp.where(lane < LANES // 2, 0.0, folded)
        return following

    over_tiles(residual, coupled_start(smooth, TOP, OWN))

    src = lax.broadcasted_iota(jnp.int32, (LANES, LANES), 0)
    dst = lax.broadcasted_iota(jnp.int32, (LANES, LANES), 1)
    found = jnp.zeros((NCY * 64, LANES), F32)
    for phase in range(PHASES):
        pick = jnp.where((phase * LANES + src) % NZ // BLK == dst, 1.0, 0.0).astype(BF16)
        for piece in halves(sums[phase].reshape(NCY * 64, LANES)):
            found = found + jnp.dot(piece, pick, preferred_element_type=F32)
    placed = found[0:64]
    for strip in range(1, NCY):
        placed = placed + lane_roll(found[strip * 64 : strip * 64 + 64], strip * NCZ)
    shares = {}
    for n, (a, c) in enumerate(PAIRED):
        add_share(shares, 1 + OFFSET[a], 1 + OFFSET[c], placed[57 + n : 58 + n])
    for a in range(3):
        for c in range(3):
            add_face(shares, 2 + OFFSET[a], 3 + OFFSET[c], placed[48 + 3 * a + c : 49 + 3 * a + c])
    part[0:ALL_ROWS, :] = operator[...]
    for n, pair in enumerate(SAME):
        if pair in shares:
            part[n : n + 1, :] += shares[pair]
    for a in range(3):
        for block in range(2):
            row = RHS_ROW + 1 + block + OFFSET[a]
            low = (2 * a + block) * 8
            part[row : row + 1, :] += jnp.sum(placed[low : low + 8], axis=0, keepdims=True)
    for n in range(1, part.shape[0] // ALL_ROWS):
        part[n * ALL_ROWS : n * ALL_ROWS + ALL_ROWS, :] = part[0:ALL_ROWS, :]
    for copy in sent:
        copy.wait()


def presmooth(count, got_a, got_b, raw, tx, ty, tz, dg, w0, w1, w2, operator):
    results = pl.pallas_call(
        presmooth_kernel,
        out_shape=(padded(),) * 4
        + (padded_out(),) * 9
        + (jax.ShapeDtypeStruct((count * ALL_ROWS, LANES), F32),)
        + (payload(),) * 2,
        in_specs=in_vmem(11),
        out_specs=tuple(in_vmem(4) + in_hbm(9) + in_vmem(3)),
        input_output_aliases={3: 0, 4: 1, 5: 2, 6: 3},
        scratch_shapes=[padded()] * 4
        + [
            vmem((PHASES, NCY, 64, LANES)),
            vmem((PAIR * 24, LANES)),
            vmem((TILES * 16, LANES)),
        ]
        + tails()
        + [semaphores(9)],
        compiler_params=params(16),
    )(got_a, got_b, raw, tx, ty, tz, dg, w0, w1, w2, operator)
    return results[4:]


def regrouped(ref, dst, shift, index, load):
    lane = lanes_of(OWN)
    rolled = {}

    def piece(quarter, t):
        offset = 3200 * quarter + NZ * shift - NZ * quarter
        first, turn = (t * LANES + offset) // LANES, offset % LANES

        def source(tile):
            tile = min(max(tile, 0), TILES - 1)
            key = (tile, turn)
            if key not in rolled:
                value = load(ref, tile)
                rolled[key] = lane_roll(value, -turn) if turn else value
            return rolled[key]

        if quarter * GROUP + shift < 0 or quarter * GROUP + shift >= 4 * GROUP:
            return None
        low_lane, high_lane = max(0, quarter * NZ - t * LANES), min(LANES, (quarter + 1) * NZ - t * LANES)
        if turn == 0 or high_lane <= LANES - turn:
            return source(first)
        if low_lane >= LANES - turn:
            return source(first + 1)
        return jnp.where(lane < LANES - turn, source(first), source(first + 1))

    for t in range(LT):
        first = t * LANES // NZ
        last = (t * LANES + LANES - 1) // NZ
        value = piece(first, t)
        if last != first:
            other = piece(last, t)
            value = jnp.zeros((OWN, LANES), F32) if value is None else value
            other = jnp.zeros((OWN, LANES), F32) if other is None else other
            value = jnp.where(lane < last * NZ - t * LANES, value, other)
        elif value is None:
            value = jnp.zeros((OWN, LANES), F32)
        dst[index, t, 0:OWN, :] = value
        dst[index, t, OWN:PAD, :] = jnp.zeros((PAD - OWN, LANES), F32)


def assemble_kernel(
    rhs_in, accum_in, x_in, y_in, z_in, center_in, lower_in, upper_in, inverse, before,
    out, raw, tx_n, ty_n, tz_n, dg_n, w0_n, w1_n, w2_n,
    rhs_v, accum_v, x_v, y_v, z_v, center_v, lower_v, upper_v,
    w, tx, ty, tz, dg, fields, rows_in, found, sems,
):
    wait = stream(
        (rhs_in, accum_in, x_in, y_in, z_in, center_in, lower_in, upper_in),
        (rhs_v, accum_v, x_v, y_v, z_v, center_v, lower_v, upper_v),
        sems,
    )
    weights = (w0_n, w1_n, w2_n)
    lane = lanes_of(OWN)

    def load(t, i, carry):
        z_before, y_before, y_second = carry
        for ref, src in zip(weights, (center_v, lower_v, upper_v)):
            ref[span(t, TOP, OWN), :] = own(src, t)
            ref[span(t, TOP + OWN, 4), :] = jnp.zeros((4, LANES), F32)
        z_pos = (i * LANES + lane) % NZ
        cells = t * LANES + lane
        here = span(t, TOP, OWN)
        x, y, z = own(x_v, t), own(y_v, t), own(z_v, t)
        y_inner = jnp.where(cells < PLANE - NZ, y, 0.0)
        z_inner = jnp.where(z_pos != NZ - 1, z, 0.0)
        z_rolled = lane_roll(z_inner, 1)
        y_rolled = lane_roll(y_inner, NZ - LANES)
        tx_n[span(t, 0, TOP), :] = jnp.zeros((TOP, LANES), F32)
        tx_n[here, :] = x
        ty_n[here, :] = y_inner
        tz_n[here, :] = z_inner
        total = own(accum_v, t) + x + tx_n[span(t, TOP - 1, OWN), :]
        total = total + y + jnp.where(lane < NZ - LANES, y_second, y_before)
        total = total + z + jnp.where(lane == 0, z_before, z_rolled)
        dg_n[here, :] = total
        raw[here, :] = rhs_v[:, at(t)]
        return z_rolled, y_rolled, y_before

    zero = lanes_of(OWN).astype(F32) * 0.0
    over_tiles(load, (zero, zero, zero), wait)

    def plain(ref, tile):
        return ref[tile * PAD + TOP : tile * PAD + TOP + OWN, :]

    for g in range(GROUP):
        regrouped(tx_n, tx, g, g, plain)
        regrouped(ty_n, ty, g, g, plain)
        regrouped(tz_n, tz, g, g, plain)
        regrouped(dg_n, dg, g, g, plain)
    for g in range(GROUP + 1):
        for a, weight in enumerate(weights):
            regrouped(weight, w.at[a], g, g, plain)

    lane8 = lanes_of(8)

    def combo(index, carry):
        half = index // (LT * 3)
        t = (index // 3) % LT
        low = (index % 3) * 8
        t_next = jnp.minimum(t + 1, LT - 1)
        same = pl.ds(pl.multiple_of(low, 8), 8)
        after = pl.ds(low + 1, 8)
        d_sum = [None] * 6
        x_sum = [None] * 9
        z_sum = [None] * 9
        for step in range(BLK):
            g = half * BLK + step
            here = [w[a, g, t, same, :] for a in range(3)]
            x_up = [w[a, g, t, after, :] for a in range(3)]
            y_up = [w[a, g + 1, t, same, :] for a in range(3)]
            z_up = [
                jnp.where(
                    lane8 == LANES - 1,
                    lane_roll(w[a, g, t_next, same, :], -1),
                    lane_roll(here[a], -1),
                )
                for a in range(3)
            ]
            d_t, x_t = dg[g, t, same, :], tx[g, t, same, :]
            y_t, z_t = ty[g, t, same, :], tz[g, t, same, :]
            d_w = [d_t * v for v in here]
            x_w = [x_t * v for v in here]
            y_w = [y_t * v for v in here]
            z_w = [z_t * v for v in here]
            for n, (a, c) in enumerate(PAIRED):
                term = d_w[a] * here[c]
                if step < BLK - 1:
                    cross = y_w[a] * y_up[c]
                    cross = cross + (cross if a == c else y_w[c] * y_up[a])
                    term = term - cross
                d_sum[n] = term if d_sum[n] is None else d_sum[n] + term
            for a in range(3):
                for c in range(3):
                    n = 3 * a + c
                    x_term = x_w[a] * x_up[c]
                    z_term = z_w[a] * z_up[c]
                    x_sum[n] = x_term if x_sum[n] is None else x_sum[n] + x_term
                    z_sum[n] = z_term if z_sum[n] is None else z_sum[n] + z_term
                    if step == BLK - 1:
                        fields[24 + n, half, t, same, :] = y_w[a] * y_up[c]
        for n in range(6):
            fields[n, half, t, same, :] = d_sum[n]
        for n in range(9):
            fields[6 + n, half, t, same, :] = x_sum[n]
            fields[15 + n, half, t, same, :] = z_sum[n]
        return carry

    lax.fori_loop(0, 2 * LT * 3, combo, 0)

    row8 = rows_of(8)

    def fold(index, carry):
        half = index // LT
        t = index % LT
        cols = pl.ds(pl.multiple_of(half * LANES, LANES), LANES)

        def tiles_of(n):
            return [fields[n, half, t, 8 * s : 8 * s + 8, :] for s in range(3)]

        def blocks(v, first):
            return (
                v[0] + jnp.where(row8 < first, v[1], 0.0),
                jnp.where(row8 >= 2, v[1], 0.0) + v[2],
            )

        x_tiles = [tiles_of(6 + n) for n in range(9)]
        x_in = [blocks(v, 1) for v in x_tiles]
        for n, (a, c) in enumerate(PAIRED):
            both = blocks(tiles_of(n), 2)
            for s in range(2):
                value = both[s] - x_in[3 * a + c][s] - x_in[3 * c + a][s]
                rows_in[t, 16 * n + 8 * s : 16 * n + 8 * s + 8, cols] = value
        for n in range(9):
            rows_in[t, 96 + 8 * n : 104 + 8 * n, cols] = jnp.where(row8 == 1, x_tiles[n][1], 0.0)
            for first, base in ((24, 168), (15, 312)):
                both = blocks(tiles_of(first + n), 2)
                for s in range(2):
                    low = base + 16 * n + 8 * s
                    rows_in[t, low : low + 8, cols] = both[s]
        return carry

    lax.fori_loop(0, 2 * LT, fold, 0)

    src = lax.broadcasted_iota(jnp.int32, (2 * LANES, 2 * LANES), 0)
    dst = lax.broadcasted_iota(jnp.int32, (2 * LANES, 2 * LANES), 1)
    total = jnp.zeros((456, 2 * LANES), F32)
    for t in range(LT):
        place = t * LANES + src % LANES
        coarse = place // NZ * 2 * NCZ + src // LANES * NCZ + place % NZ // BLK
        column = coarse + jnp.where(place % BLK == BLK - 1, LANES, 0)
        pick = jnp.where(column == dst, 1.0, 0.0).astype(BF16)
        for piece in halves(rows_in[t]):
            total = total + jnp.dot(piece, pick, preferred_element_type=F32)
    found[0:57, :] = jnp.sum(total.reshape(57, 8, 2 * LANES), axis=1)

    def both(row):
        return found[row : row + 1, 0:LANES] + found[row : row + 1, LANES:]

    def inside(row):
        return found[row : row + 1, 0:LANES]

    def crossing(row):
        return found[row : row + 1, LANES:]

    shares, y_shares, z_shares = {}, {}, {}
    for block in range(2):
        rows = [1 + block + OFFSET[a] for a in range(3)]
        for n, (a, c) in enumerate(PAIRED):
            value = both(2 * n + block)
            value = value - inside(39 + 2 * (3 * a + c) + block) - inside(39 + 2 * (3 * c + a) + block)
            add_share(shares, rows[a], rows[c], value)
        for a in range(3):
            for c in range(3):
                n = 3 * a + c
                pair = (rows[a], rows[c])
                for kept, value in (
                    (y_shares, both(21 + 2 * n + block)),
                    (z_shares, crossing(39 + 2 * n + block)),
                ):
                    kept[pair] = kept[pair] - value if pair in kept else -value
                if block == 0:
                    add_face(shares, 1 + OFFSET[a], 2 + OFFSET[c], both(12 + n))
    out[...] = jnp.zeros_like(out)
    for first, pairs, kept in ((0, SAME, shares), (Y_ROW, ACROSS, y_shares), (Z_ROW, ACROSS, z_shares)):
        for n, pair in enumerate(pairs):
            if pair in kept:
                out[first + n : first + n + 1, :] = kept[pair]
    out[INVERSE_ROW : INVERSE_ROW + 2, :] = inverse[...]


def assemble(rhs, accum, trans_x, trans_y, trans_z, center, lower, upper, inverse, before):
    slab = (LT, PAD, LANES)
    return pl.pallas_call(
        assemble_kernel,
        out_shape=(vmem((ALL_ROWS, LANES)),) + (padded(),) * 8,
        in_specs=in_hbm(8) + in_vmem(1) + [pl.BlockSpec(memory_space=pl.ANY)],
        out_specs=tuple(in_vmem(9)),
        scratch_shapes=[cells(F32)]
        + [cells()] * 7
        + [
            vmem((3, GROUP + 1) + slab),
            vmem((GROUP,) + slab),
            vmem((GROUP,) + slab),
            vmem((GROUP,) + slab),
            vmem((GROUP,) + slab),
            vmem((33, 2, LT, 24, LANES)),
            vmem((LT, 456, 2 * LANES)),
            vmem((57, 2 * LANES)),
            semaphores(8, PAIRS),
        ],
        compiler_params=params(32),
    )(rhs, accum, trans_x, trans_y, trans_z, center, lower, upper, inverse, before)


EDGE = 8


def coarse_solve(count, gathered, same, same_t, y_mat, y_mat_t, z_mat, z_mat_t, inv, rhs, e, e_y, e_z):
    rows = 2 * count
    here = pl.ds(EDGE, rows)
    for ref in (same, y_mat, z_mat, inv, rhs, e, e_y, e_z):
        ref[...] = jnp.zeros_like(ref)

    def share(row):
        return gathered[pl.ds(row, count, ALL_ROWS), :]

    def add(ref, u, value):
        place = pl.ds(EDGE - 1 + u, count, 2)
        ref[place, :] = ref[place, :] + value

    for n, (u, v) in enumerate(SAME):
        add(same.at[v - u], u, share(n))
    for n, (u, v) in enumerate(ACROSS):
        add(y_mat.at[v - u + 2], u, share(Y_ROW + n))
        add(z_mat.at[v - u + 2], u, share(Z_ROW + n))
    for u in range(4):
        add(rhs, u, share(RHS_ROW + u))
    for block in range(2):
        inv[pl.ds(EDGE + block, count, 2), :] = OMEGA_COARSE * share(INVERSE_ROW + block)
    for step in range(1, 4):
        same_t[step - 1] = same[step, pl.ds(EDGE - step, rows), :]
    for step in range(-2, 3):
        y_mat_t[step + 2] = y_mat[step + 2, pl.ds(EDGE - step, rows), :]
        z_mat_t[step + 2] = z_mat[step + 2, pl.ds(EDGE - step, rows), :]
    e[here, :] = inv[here, :] * rhs[here, :]

    def one(index, carry):
        at_step = {step: e[pl.ds(EDGE + step, rows), :] for step in range(-3, 4)}
        e_y[here, :] = lane_roll(at_step[0], -NCZ)
        e_z[here, :] = lane_roll(at_step[0], -1)
        image = same[0, here, :] * at_step[0]
        for step in range(1, 4):
            image = image + same[step, here, :] * at_step[step] + same_t[step - 1] * at_step[-step]
        y_back = z_back = None
        for step in range(-2, 3):
            y_term = y_mat_t[step + 2] * at_step[-step]
            z_term = z_mat_t[step + 2] * at_step[-step]
            y_back = y_term if y_back is None else y_back + y_term
            z_back = z_term if z_back is None else z_back + z_term
        image = image + lane_roll(y_back, NCZ) + lane_roll(z_back, 1)
        for step in range(-2, 3):
            place = pl.ds(EDGE + step, rows)
            image = image + y_mat[step + 2, here, :] * e_y[place, :]
            image = image + z_mat[step + 2, here, :] * e_z[place, :]
        e[here, :] = at_step[0] + inv[here, :] * (rhs[here, :] - image)
        return carry

    lax.fori_loop(0, CSW - 1, one, 0)


def finish_kernel(
    count, gathered_rows, got_a, got_b, smooth_in, tx_in, ty_in, tz_in, k_in, b_in, w0_in, w1_in, w2_in,
    out, update,
    smooth, tx, ty, tz, k, b, w0, w1, w2,
    same, same_t, y_mat, y_mat_t, z_mat, z_mat_t, inv, rhs, e, e_y, e_z, strips, spread, first, second, tail_a, tail_b, sems,
):
    weights = (w0, w1, w2)
    coming = copies(
        (smooth_in, w0_in, w1_in, w2_in, tx_in, ty_in, tz_in, k_in, b_in),
        (smooth, w0, w1, w2, tx, ty, tz, k, b),
        sems,
    )
    coarse_solve(
        count, gathered_rows, same, same_t, y_mat, y_mat_t, z_mat, z_mat_t, inv, rhs, e, e_y, e_z
    )
    base = EDGE + 2 * lax.axis_index("gx")
    update[...] = e[pl.ds(base, 2), :]
    near = {s: e[pl.ds(base + s, 1), :] for s in range(-2, 4)}
    row = rows_of(PAD)
    lane = lanes_of(PAD)
    for a, s in enumerate((0, -1, 1)):
        value = jnp.where(row < TOP + BLK, near[s], near[s + 1])
        value = jnp.where(row < TOP, near[s - 1], value)
        value = jnp.where(row >= TOP + OWN, near[s + 2], value)
        high = value.astype(BF16).astype(F32)
        rest = value - high
        low = rest.astype(BF16).astype(F32)
        rest = rest - low
        for strip in range(NCY):
            turned = lane_roll(high, -strip * NCZ)
            turned = jnp.where(lane < NCZ, turned, lane_roll(low, (1 - strip) * NCZ))
            turned = jnp.where(lane < 2 * NCZ, turned, lane_roll(rest, (2 - strip) * NCZ))
            turned = jnp.where(lane < 3 * NCZ, turned, 0.0)
            strips[a, strip] = turned.astype(BF16)
    src = lax.broadcasted_iota(jnp.int32, (LANES, LANES), 0)
    dst = lax.broadcasted_iota(jnp.int32, (LANES, LANES), 1)
    flat = strips[...].reshape(3 * NCY * PAD, LANES)
    for phase in range(PHASES):
        pick = jnp.where((phase * LANES + dst) % NZ // BLK == src % NCZ, 1.0, 0.0).astype(BF16)
        got = jnp.dot(flat, pick, preferred_element_type=F32)
        spread[phase] = got.reshape(3, NCY, PAD, LANES)

    for copy in coming:
        copy.wait()
    both = received(got_a, got_b, tail_a, tail_b)
    for q in range(WHOLE + 1):
        size = 16 if q < WHOLE else REST
        values = [both(n, q) for n in range(PLANES)]
        for side, rows in ((0, (7, 6, 5)), (1, (28, 29, 30))):
            got = [v[side] for v in values]
            for n, row in enumerate(rows):
                smooth[plane(smooth, row, q, size), :] = got[2 * n] + got[2 * n + 1]
                for a, w in enumerate(weights):
                    w[plane(w, row, q, size), :] = got[6 + 3 * a + n]

    def prolong(t, i, carry):
        n = t // PAIR
        phase = i % PHASES
        here = span(t, 0, PAD)
        total = smooth[here, :]
        for a, w in enumerate(weights):
            if i == PAIR // 2:
                values = jnp.where(
                    lane < LANES // 2, spread[phase, a, 2 * n], spread[phase, a, 2 * n + 1]
                )
            else:
                values = spread[phase, a, 2 * n + (1 if i > PAIR // 2 else 0)]
            total = total + w[here, :] * values
        first[here, :] = total
        return carry

    over_tiles(prolong, 0)
    sweep(first, second, tx, ty, tz, k, b, 6, 24)
    sweep(second, first, tx, ty, tz, k, b, 7, 22)

    def last(t, i, carry):
        total, after = coupled(first, tx, ty, tz, t, TOP, OWN, carry)
        here = span(t, TOP, OWN)
        out[:, at(t)] = b[here, :] + (1.0 - OMEGA_FINE) * carry[0] + k[here, :] * total
        return after

    over_tiles(last, coupled_start(first, TOP, OWN))


def finish(gathered_rows, got_a, got_b, smooth, tx, ty, tz, k, b, w0, w1, w2):
    count = gathered_rows.shape[0] // ALL_ROWS
    rows = 2 * count

    def kernel(*refs):
        finish_kernel(count, *refs)

    return pl.pallas_call(
        kernel,
        out_shape=(
            jax.ShapeDtypeStruct((OWN, PLANE), F32),
            jax.ShapeDtypeStruct((2, LANES), F32),
        ),
        in_specs=in_vmem(3) + in_hbm(9),
        out_specs=tuple(in_vmem(2)),
        scratch_shapes=[padded()] * 9
        + [
            vmem((4, rows + 2 * EDGE, LANES)),
            vmem((3, rows, LANES)),
            vmem((5, rows + 2 * EDGE, LANES)),
            vmem((5, rows, LANES)),
            vmem((5, rows + 2 * EDGE, LANES)),
            vmem((5, rows, LANES)),
        ]
        + [vmem((rows + 2 * EDGE, LANES))] * 5
        + [
            vmem((3, NCY, PAD, LANES), BF16),
            vmem((PHASES, 3, NCY, PAD, LANES)),
            vmem((TILES * PAD, LANES)),
            vmem((TILES * PAD, LANES)),
        ]
        + tails()
        + [semaphores(9)],
        compiler_params=params(58),
    )(gathered_rows, got_a, got_b, smooth, tx, ty, tz, k, b, w0, w1, w2)


def swapped(pay_a, pay_b):
    count = lax.axis_size("gx")
    got_a = lax.ppermute(pay_a, "gx", [(i, i ^ 1) for i in range(count)])
    inner = [(i, i + 1 if i % 2 else i - 1) for i in range(1, count - 1)]
    return got_a, lax.ppermute(pay_b, "gx", inner)


def spread_out(rows):
    count = lax.axis_size("gx")
    each = rows.shape[0] // count
    got = lax.all_to_all(rows.reshape(count, each, LANES), "gx", 0, 0)
    return got.reshape(count * each, LANES)


def per_device(
    rhs, accumulation, trans_x, trans_y, trans_z, basis_center, basis_side, coarse_inverse
):
    count = lax.axis_size("gx")
    pay_a, pay_b = prepare(
        rhs, accumulation, trans_x, trans_y, trans_z, basis_center, basis_side[:, 0]
    )
    got_a, got_b = swapped(pay_a, pay_b)
    operator, *own_fields = assemble(
        rhs, accumulation, trans_x, trans_y, trans_z, basis_center, basis_side[0], basis_side[1],
        coarse_inverse, pay_b,
    )
    *kept, part, pay_a, pay_b = presmooth(count, got_a, got_b, *own_fields, operator)
    got_a, got_b = swapped(pay_a, pay_b)
    gathered = spread_out(part)
    tx, ty, tz, k, b, smooth, w0, w1, w2 = kept
    return finish(gathered, got_a, got_b, smooth, tx, ty, tz, k, b, w0, w1, w2)


def solution(mesh):
    both = ("grp", "gx")
    cells = P(both, None)
    return jax.shard_map(
        per_device,
        mesh=mesh,
        in_specs=(cells,) * 6 + (P(None, both, None), cells),
        out_specs=(cells, cells),
        check_vma=False,
    )
```

profile of v0, /device:TPU:9, one launch (start us, length us, event | category | flops | bytes accessed | tf_op | source)
XLA Modules:
  0.0 74.8 jit_solution(16629524406213655181)
XLA Ops:
  0.6 1.5 %slice_bitcast_fusion.first_side = bf16[2,12800]{1,0:T(2,128)(2,1)} fusion(bf16[2,20,12800]{2,0,1:T(2,128)(2,1)} %param.14), kind=kLoop, calls=%fused_computation.2 | loop fusion | bytes 102400 | tf_op jit(solution)/shard_map/squeeze | solution.py:941
  2.1 0.0 copy-start.8
  2.1 4.7 %shard_map.95 = (bf16[1600,128]{1,0:T(8,128)(2,1)}, bf16[1600,128]{1,0:T(8,128)(2,1)}) custom-call(f32[20,12800]{1,0:T(8,128)} %rhs_in.1, bf16[20,12800]{1,0:T(8,128)(2,1)} %accum_in.1, bf16[20,12800]{1,0:T(8,128)(2,1)} %x_in.1, bf16[20,12800]{1,0:T(8,128)(2,1)} %y_in.1, bf16[20,12800]{1,0:T(8,128)(2,1)} %z_in.1, bf16[20,12800]{1,0:T(8,128)(2,1)} %center_in.1, ...), custom_call_target="tpu_custom_call" | custom-call | tf_op jit(solution)/shard_map/pallas_call | solution.py:311
  6.7 0.7 collective-permute-start
  7.5 3.0 %collective-permute-start.1 = (bf16[1600,128]{1,0:T(8,128)(2,1)}, bf16[1600,128]{1,0:T(8,128)(2,1)S(1)}, u32[]{:S(2)}, u32[]{:S(2)}) collective-permute-start(bf16[1600,128]{1,0:T(8,128)(2,1)} %get-tuple-element.26.before), channel_id=1, source_target_pairs={{1,2},{2,1},{3,4},{4,3},{5,6},{6,5},{7,8},{8,7},{9,10},{10,9},{11,... | collective-permute-start | bytes 1228808 | tf_op jit(solution)/shard_map/ppermute | solution.py:926
  10.5 0.0 copy-done.8
  10.6 0.0 copy-start.4
  10.6 0.0 copy-start.5
  10.6 0.0 copy-start.6
  10.6 1.5 %fusion = (bf16[1,20,12800]{2,0,1:T(2,128)(2,1)S(1)}, bf16[1,20,12800]{2,0,1:T(2,128)(2,1)S(1)}) fusion(bf16[2,20,12800]{2,0,1:T(2,128)(2,1)S(1)} %copy-done.8), kind=kLoop, calls=%fused_computation.3 | loop fusion | bytes 2048000 | tf_op jit(solution)/shard_map/slice | solution.py:945
  12.1 0.0 copy-start
  12.1 0.0 copy-start.1
  12.1 0.0 copy-start.2
  12.1 0.0 copy-start.3
  12.1 0.0 copy-start.7
  12.1 0.2 copy_bitcast_fusion
  12.3 0.0 copy-done.4
  12.3 0.0 copy-done.5
  12.3 0.0 copy-done.6
  12.3 1.0 %copy-done = f32[20,12800]{1,0:T(8,128)S(1)} copy-done((f32[20,12800]{1,0:T(8,128)S(1)}, f32[20,12800]{1,0:T(8,128)}, u32[]{:S(2)}) %copy-start) | copy-done | bytes 1024024
  13.4 0.2 copy-done.1
  13.5 0.2 copy-done.2
  13.7 0.2 copy-done.3
  13.9 0.0 copy-done.7
  13.9 14.1 %shard_map.96 = (f32[48,128]{1,0:T(8,128)S(1)}, f32[3200,128]{1,0:T(8,128)S(1)}, f32[3200,128]{1,0:T(8,128)S(1)}, f32[3200,128]{1,0:T(8,128)S(1)}, f32[3200,128]...) custom-call(f32[20,12800]{1,0:T(8,128)S(1)} %copy-done, ...), custom_call_target="tpu_custom_call" | custom-call | tf_op jit(solution)/shard_map/pallas_call | solution.py:723
  28.0 0.0 collective-permute-done.got_a
  28.0 0.0 collective-permute-done.1.got_b
  28.0 9.4 %shard_map.97 = (f32[3200,128]{1,0:T(8,128)S(1)}, f32[3200,128]{1,0:T(8,128)S(1)}, f32[3200,128]{1,0:T(8,128)S(1)}, f32[3200,128]{1,0:T(8,128)S(1)}, f32[3200,12...) custom-call(bf16[1600,128]{1,0:T(8,128)(2,1)S(1)} %collective-permut, ...), custom_call_target="tpu_custom_call", output_to_operand_aliasing={{0}: (3, {}), {1}: (4, {}), {2}: (5, {}), {3}: (6, {})} | custom-call | tf_op jit(solution)/shard_map/pallas_call | solution.py:469
  37.4 5.4 %all-to-all-start = ((f32[16,48,128]{2,1,0:T(8,128)}), f32[16,48,128]{2,1,0:T(8,128)S(1)}, u32[]{:S(2)}, u32[]{:S(2)}) async-start(f32[16,48,128]{2,1,0:T(8,128)} %bitcast.3), calls=%async_computation | async-start | bytes 786432 | tf_op jit(solution)/shard_map/all_to_all | solution.py:932
  42.9 0.4 collective-permute-start.2
  43.2 3.3 %collective-permute-start.3 = (bf16[1600,128]{1,0:T(8,128)(2,1)S(1)}, bf16[1600,128]{1,0:T(8,128)(2,1)S(1)}, u32[]{:S(2)}, u32[]{:S(2)}) collective-permute-start(bf16[1600,128]{1,0:T(8,128)(2,1)S(1)} %get-tuple-element.38), channel_id=1, source_target_pairs={{1,2},{2,1},{3,4},{4,3},{5,6},{6,5},{7,8},{8,7},{9,10},{10,9},{11,... | collective-permute-start | bytes 1228808 | tf_op jit(solution)/shard_map/ppermute | solution.py:926
  46.5 0.0 collective-permute-done.2.refs_1_
  46.5 0.0 copy-start.10
  46.5 12.7 %collective-permute-done.3.refs_2_ = bf16[1600,128]{1,0:T(8,128)(2,1)S(1)} collective-permute-done((bf16[1600,128]{1,0:T(8,128)(2,1)S(1)}, bf16[1600,128]{1,0:T(8,128)(2,1)S(1)}, u32[]{:S(2)}, u32[]{:S(2)}) %collective-permute-start.3) | collective-permute-done | bytes 409632 | tf_op jit(solution)/shard_map/ppermute | solution.py:926
  59.3 0.0 copy-start.11
  59.3 0.0 all-to-all-done
  59.3 0.0 copy-start.9
  59.3 0.0 copy-done.10
  59.3 0.8 %copy-done.11 = bf16[1600,128]{1,0:T(8,128)(2,1)} copy-done((bf16[1600,128]{1,0:T(8,128)(2,1)}, bf16[1600,128]{1,0:T(8,128)(2,1)S(1)}, u32[]{:S(2)}) %copy-start.11) | copy-done | bytes 409624
  60.1 0.1 copy-done.9
  60.2 14.4 %shard_map.98 = (f32[20,12800]{1,0:T(8,128)}, f32[2,128]{1,0:T(2,128)}) custom-call(f32[768,128]{1,0:T(8,128)} %bitcast.8, bf16[1600,128]{1,0:T(8,128)(2,1)} %copy-done.10, bf16[1600,128]{1,0:T(8,128)(2,1)} %copy-done.11, f32[3200,128]{1,0:T(8,128)} %get-tuple-element.39.refs_3_, f32[3200,128]{1,0:T(8,128)} %get-tuple-element.40.refs_4_, ...), custom_call_target="tpu_custom_call" | custom-call | tf_op jit(solution)/shard_map/pallas_call | solution.py:892
Async XLA Ops:
  2.1 8.5 %copy-start.8 = (bf16[2,20,12800]{2,0,1:T(2,128)(2,1)S(1)}, bf16[2,20,12800]{2,0,1:T(2,128)(2,1)}, u32[]{:S(2)}) copy-start(bf16[2,20,12800]{2,0,1:T(2,128)(2,1)} %param.14) | copy-start | bytes 3072004
  6.7 21.3 %collective-permute-start = (bf16[1600,128]{1,0:T(8,128)(2,1)}, bf16[1600,128]{1,0:T(8,128)(2,1)S(1)}, u32[]{:S(2)}, u32[]{:S(2)}) collective-permute-start(bf16[1600,128]{1,0:T(8,128)(2,1)} %get-tuple-element.25), channel_id=1, source_target_pairs={{0,1},{1,0},{2,3},{3,2},{4,5},{5,4},{6,7},{7,6},{8,9},{9,8},{10,11... | collective-permute-start | bytes 1228808 | tf_op jit(solution)/shard_map/ppermute | solution.py:924
  7.5 20.5 %collective-permute-start.1 = (bf16[1600,128]{1,0:T(8,128)(2,1)}, bf16[1600,128]{1,0:T(8,128)(2,1)S(1)}, u32[]{:S(2)}, u32[]{:S(2)}) collective-permute-start(bf16[1600,128]{1,0:T(8,128)(2,1)} %get-tuple-element.26.before), channel_id=1, source_target_pairs={{1,2},{2,1},{3,4},{4,3},{5,6},{6,5},{7,8},{8,7},{9,10},{10,9},{11,... | collective-permute-start | bytes 1228808 | tf_op jit(solution)/shard_map/ppermute | solution.py:926
  10.6 1.7 %copy-start.4 = (bf16[20,12800]{1,0:T(8,128)(2,1)S(1)}, bf16[20,12800]{1,0:T(8,128)(2,1)}, u32[]{:S(2)}) copy-start(bf16[20,12800]{1,0:T(8,128)(2,1)} %z_in.1) | copy-start | bytes 1536004
  10.6 1.7 %copy-start.5 = (bf16[20,12800]{1,0:T(8,128)(2,1)S(1)}, bf16[20,12800]{1,0:T(8,128)(2,1)}, u32[]{:S(2)}) copy-start(bf16[20,12800]{1,0:T(8,128)(2,1)} %center_in.1) | copy-start | bytes 1536004
  10.6 1.7 %copy-start.6 = (bf16[1600,128]{1,0:T(8,128)(2,1)S(1)}, bf16[1600,128]{1,0:T(8,128)(2,1)}, u32[]{:S(2)}) copy-start(bf16[1600,128]{1,0:T(8,128)(2,1)} %get-tuple-element.26.before) | copy-start | bytes 1228804
  12.1 1.3 %copy-start = (f32[20,12800]{1,0:T(8,128)S(1)}, f32[20,12800]{1,0:T(8,128)}, u32[]{:S(2)}) copy-start(f32[20,12800]{1,0:T(8,128)} %rhs_in.1) | copy-start | bytes 3072004
  12.1 1.4 %copy-start.1 = (bf16[20,12800]{1,0:T(8,128)(2,1)S(1)}, bf16[20,12800]{1,0:T(8,128)(2,1)}, u32[]{:S(2)}) copy-start(bf16[20,12800]{1,0:T(8,128)(2,1)} %accum_in.1) | copy-start | bytes 1536004
  12.1 1.6 %copy-start.2 = (bf16[20,12800]{1,0:T(8,128)(2,1)S(1)}, bf16[20,12800]{1,0:T(8,128)(2,1)}, u32[]{:S(2)}) copy-start(bf16[20,12800]{1,0:T(8,128)(2,1)} %x_in.1) | copy-start | bytes 1536004
  12.1 1.8 %copy-start.3 = (bf16[20,12800]{1,0:T(8,128)(2,1)S(1)}, bf16[20,12800]{1,0:T(8,128)(2,1)}, u32[]{:S(2)}) copy-start(bf16[20,12800]{1,0:T(8,128)(2,1)} %y_in.1) | copy-start | bytes 1536004
  12.1 1.8 %copy-start.7 = (f32[2,128]{1,0:T(2,128)S(1)}, f32[2,128]{1,0:T(2,128)}, u32[]{:S(2)}) copy-start(f32[2,128]{1,0:T(2,128)} %inverse.1) | copy-start | bytes 3076
  37.4 21.9 %all-to-all-start = ((f32[16,48,128]{2,1,0:T(8,128)}), f32[16,48,128]{2,1,0:T(8,128)S(1)}, u32[]{:S(2)}, u32[]{:S(2)}) async-start(f32[16,48,128]{2,1,0:T(8,128)} %bitcast.3), calls=%async_computation | async-start | bytes 786432 | tf_op jit(solution)/shard_map/all_to_all | solution.py:932
  42.9 3.7 %collective-permute-start.2 = (bf16[1600,128]{1,0:T(8,128)(2,1)S(1)}, bf16[1600,128]{1,0:T(8,128)(2,1)S(1)}, u32[]{:S(2)}, u32[]{:S(2)}) collective-permute-start(bf16[1600,128]{1,0:T(8,128)(2,1)S(1)} %get-tuple-element.37), channel_id=1, source_target_pairs={{0,1},{1,0},{2,3},{3,2},{4,5},{5,4},{6,7},{7,6},{8,9},{9,8},{10,11... | collective-permute-start | bytes 1228808 | tf_op jit(solution)/shard_map/ppermute | solution.py:924
  43.2 16.1 %collective-permute-start.3 = (bf16[1600,128]{1,0:T(8,128)(2,1)S(1)}, bf16[1600,128]{1,0:T(8,128)(2,1)S(1)}, u32[]{:S(2)}, u32[]{:S(2)}) collective-permute-start(bf16[1600,128]{1,0:T(8,128)(2,1)S(1)} %get-tuple-element.38), channel_id=1, source_target_pairs={{1,2},{2,1},{3,4},{4,3},{5,6},{6,5},{7,8},{8,7},{9,10},{10,9},{11,... | collective-permute-start | bytes 1228808 | tf_op jit(solution)/shard_map/ppermute | solution.py:926
  46.5 12.8 %copy-start.10 = (bf16[1600,128]{1,0:T(8,128)(2,1)}, bf16[1600,128]{1,0:T(8,128)(2,1)S(1)}, u32[]{:S(2)}) copy-start(bf16[1600,128]{1,0:T(8,128)(2,1)S(1)} %collective-permute-done.2.refs_1_) | copy-start | bytes 1228804
  59.3 0.8 %copy-start.11 = (bf16[1600,128]{1,0:T(8,128)(2,1)}, bf16[1600,128]{1,0:T(8,128)(2,1)S(1)}, u32[]{:S(2)}) copy-start(bf16[1600,128]{1,0:T(8,128)(2,1)S(1)} %collective-permute-done.3.refs_2_) | copy-start | bytes 1228804
  59.3 0.9 %copy-start.9 = (f32[16,48,128]{2,1,0:T(8,128)}, f32[16,48,128]{2,1,0:T(8,128)S(1)}, u32[]{:S(2)}) copy-start(f32[16,48,128]{2,1,0:T(8,128)S(1)} %all-to-all-done) | copy-start | bytes 1179652
where the time goes:
time: 75.2 us; the launch traced here: 74.8 us
  Pallas kernels  42.6 us (57%)
  starting transfers between devices  12.9 us (17%)
  waiting for transfers between devices  12.8 us (17%)
  local copies, waits for them, and re-layouts  5.57 us (7%)
  between operations  0.98 us (1%)
    pallas_call x1, Pallas kernels, finish(): pl.pallas_call(kernel, out_shape=(jax.ShapeDtypeStruct((OWN, PLANE), F32)...  14.4 us
    pallas_call x1, Pallas kernels, assemble(): pl.pallas_call(assemble_kernel, out_shape=(vmem((ALL_ROWS, LANES)),) + (p...  14.1 us
    ppermute x2, waiting for transfers between devices, swapped(): return (got_a, lax.ppermute(pay_b, 'gx', inner))  12.7 us
    pallas_call x1, Pallas kernels, presmooth(): pl.pallas_call(presmooth_kernel, out_shape=(padded(),) * 4 + (padded_out(...  9.4 us
    ppermute x2, starting transfers between devices, swapped(): return (got_a, lax.ppermute(pay_b, 'gx', inner))  6.34 us
    all_to_all x1, starting transfers between devices, spread_out(): got = lax.all_to_all(rows.reshape(count, each, LANES), 'gx', 0, 0)  5.42 us
    pallas_call x1, Pallas kernels, prepare(): pl.pallas_call(prepare_kernel, out_shape=(payload(),) * 2, in_specs=in_hb...  4.65 us
    unnamed x24, local copies, waits for them, and re-layouts  2.48 us
  transfers between devices with their start and end apart: 5, of which 1 were waited for; matrix products, arithmetic and copies ran while one was open for 2% of the time, Pallas kernels for 19%

commit v1 on v0

--- a/solution.py
+++ b/solution.py
@@ -21,13 +21,19 @@
 PAIR = 25
 PAIRS = TILES // PAIR
 OWN = 20
-TOP = 8
-PAD = 32
+TOP = 3
+PAD = OWN + 2 * TOP
+HEAD = (TOP, TOP + 1, TOP + 2)
+LAST = (TOP + OWN - 1, TOP + OWN - 2, TOP + OWN - 3)
+BEFORE = (TOP - 1, TOP - 2, TOP - 3)
+BEYOND = (TOP + OWN, TOP + OWN + 1, TOP + OWN + 2)
+SPREAD = 32
 GROUP = 20
 QUARTERS = 4
 LT = QUARTERS * NZ // LANES
 PAIRED = ((0, 0), (0, 1), (0, 2), (1, 1), (1, 2), (2, 2))
-PLANES = 16
+FIRST = 17
+SECOND = 10
 WHOLE = TILES // 16
 REST = TILES % 16
 OFFSET = (0, -1, 1)
@@ -46,6 +52,12 @@
     return pltpu.CompilerParams(vmem_limit_bytes=mib << 20)
 
 
+def lasting(microseconds):
+    return pl.CostEstimate(
+        flops=0, transcendentals=0, bytes_accessed=int(3.5e6 * microseconds)
+    )
+
+
 def vmem(shape, dtype=F32):
     return pltpu.VMEM(shape, dtype)
 
@@ -59,11 +71,11 @@
 
 
 def padded():
-    return vmem((TILES * PAD, LANES))
+    return vmem((TILES * PAD + 8, LANES))
 
 
 def padded_out():
-    return pltpu.HBM((TILES * PAD, LANES), F32)
+    return pltpu.HBM((TILES * PAD + 8, LANES), F32)
 
 
 def cells(dtype=BF16):
@@ -188,7 +200,7 @@
         dst[here, :] = b[here, :] + (1.0 - OMEGA_FINE) * carry[0] + k[here, :] * total
         return after
 
-    over_tiles(body, coupled_start(src, low, count), unroll=2)
+    over_tiles(body, coupled_start(src, low, count), unroll=4)
 
 
 def plane(ref, row, q, size, stride=PAD):
@@ -201,7 +213,8 @@
 
 def send_both(pay_a, pay_b, tail_a, tail_b, right, left):
     even = parity() == 0
-    for n in range(PLANES):
+    count = len(right)
+    for n in range(count):
         for q in range(WHOLE + 1):
             size = 16 if q < WHOLE else REST
             r, l = right[n](q, size), left[n](q, size)
@@ -214,14 +227,14 @@
                 rows = slice(n * REST, n * REST + REST)
                 tail_a[rows, :] = a
                 tail_b[rows, :] = b
-    pay_a[PLANES * WHOLE * 16 :, :] = tail_a[...].astype(BF16)
-    pay_b[PLANES * WHOLE * 16 :, :] = tail_b[...].astype(BF16)
-
-
-def received(got_a, got_b, tail_a, tail_b):
+    pay_a[count * WHOLE * 16 :, :] = tail_a[...].astype(BF16)
+    pay_b[count * WHOLE * 16 :, :] = tail_b[...].astype(BF16)
+
+
+def received(count, got_a, got_b, tail_a, tail_b):
     even = parity() == 0
-    tail_a[...] = got_a[PLANES * WHOLE * 16 :, :].astype(F32)
-    tail_b[...] = got_b[PLANES * WHOLE * 16 :, :].astype(F32)
+    tail_a[...] = got_a[count * WHOLE * 16 :, :].astype(F32)
+    tail_b[...] = got_b[count * WHOLE * 16 :, :].astype(F32)
 
     def both(n, q):
         if q < WHOLE:
@@ -235,93 +248,90 @@
     return both
 
 
-def payload():
-    return jax.ShapeDtypeStruct((PLANES * TILES, LANES), BF16)
-
-
-def tails():
-    return [vmem((PLANES * REST, LANES))] * 2
+def payload_rows(count):
+    return -(-count * TILES // 16) * 16
+
+
+def payload(count):
+    return jax.ShapeDtypeStruct((payload_rows(count), LANES), BF16)
+
+
+def tails(count):
+    return [vmem((payload_rows(count) - count * WHOLE * 16, LANES))] * 2
+
+
+def low_part(f):
+    return lambda q, size: remainder(f(q, size))
 
 
 def prepare_kernel(
-    rhs, accum, trans_x, trans_y, trans_z, center, first_side, pay_a, pay_b,
-    rhs_v, accum_v, x_v, y_v, z_v, center_v, raw, tx, ty, tz, dg, basis, tail_a, tail_b, sems,
+    rhs_in, accum_in, x_in, y_in, z_in, center_in, side_in,
+    raw, tx_n, ty_n, tz_n, dg_n, w0_n, w1_n, w2_n, pay_a, pay_b,
+    rhs_v, accum_v, x_v, y_v, z_v, center_v, lower_v, upper_v, tail_a, tail_b, sems,
 ):
     wait = stream(
-        (rhs, accum, trans_x, trans_y, trans_z, center.at[0:16, :]),
-        (rhs_v, accum_v, x_v, y_v, z_v, center_v),
+        (rhs_in, accum_in, x_in, y_in, z_in, center_in, side_in.at[0], side_in.at[1]),
+        (rhs_v, accum_v, x_v, y_v, z_v, center_v, lower_v, upper_v),
         sems,
     )
-    lane = lanes_of(12)
-
-    def ends(ref, t):
-        value = own(ref, t)
-        return jnp.concatenate([value[0:8], value[16:20]], axis=0)
-
-    def body(t, i, carry):
+    weights = (w0_n, w1_n, w2_n)
+    lane = lanes_of(OWN)
+
+    def load(t, i, carry):
         z_before, y_before, y_second = carry
+        for ref, src in zip(weights, (center_v, lower_v, upper_v)):
+            ref[span(t, TOP, OWN), :] = own(src, t)
         z_pos = (i * LANES + lane) % NZ
         cells = t * LANES + lane
-        here = pl.ds(t * 24 + 8, 12)
-        x, y, z = ends(x_v, t), ends(y_v, t), ends(z_v, t)
+        here = span(t, TOP, OWN)
+        x, y, z = own(x_v, t), own(y_v, t), own(z_v, t)
         y_inner = jnp.where(cells < PLANE - NZ, y, 0.0)
         z_inner = jnp.where(z_pos != NZ - 1, z, 0.0)
         z_rolled = lane_roll(z_inner, 1)
         y_rolled = lane_roll(y_inner, NZ - LANES)
-        tx[pl.ds(t * 24, 8), :] = jnp.zeros((8, LANES), F32)
-        tx[here, :] = x
-        ty[here, :] = y_inner
-        tz[here, :] = z_inner
-        total = ends(accum_v, t) + x + tx[pl.ds(t * 24 + 7, 12), :]
+        tx_n[span(t, TOP - 1, 1), :] = jnp.zeros((1, LANES), F32)
+        tx_n[here, :] = x
+        ty_n[here, :] = y_inner
+        tz_n[here, :] = z_inner
+        total = own(accum_v, t) + x + tx_n[span(t, TOP - 1, OWN), :]
         total = total + y + jnp.where(lane < NZ - LANES, y_second, y_before)
         total = total + z + jnp.where(lane == 0, z_before, z_rolled)
-        dg[here, :] = total
-        raw[here, :] = ends(rhs_v, t)
-        basis[pl.ds(t * 8, 2), :] = first_side[:, at(t)].astype(F32)
-        basis[pl.ds(t * 8 + 2, 1), :] = center_v[:, at(t)].astype(F32)[0:1]
+        dg_n[here, :] = total
+        raw[here, :] = rhs_v[:, at(t)]
         return z_rolled, y_rolled, y_before
 
-    zero = lanes_of(12).astype(F32) * 0.0
-    over_tiles(body, (zero, zero, zero), wait)
-
-    def low_part(f):
-        return lambda q, size: remainder(f(q, size))
+    zero = lanes_of(OWN).astype(F32) * 0.0
+    over_tiles(load, (zero, zero, zero), wait)
 
     def first_sweep(row):
-        r, d = read_plane(raw, row, 24), read_plane(dg, row, 24)
+        r, d = read_plane(raw, row), read_plane(dg_n, row)
         return lambda q, size: OMEGA_FINE * r(q, size) / d(q, size)
 
-    def planes(near, second, far, x_rows):
-        r, d = read_plane(raw, near, 24), read_plane(dg, near, 24)
-        return (
-            [r, low_part(r), read_plane(raw, second, 24)]
-            + [d, low_part(d), read_plane(dg, second, 24)]
-            + [read_plane(ref, row, 24) for ref in (ty, tz) for row in (near, second)]
-            + [first_sweep(far)]
-            + [read_plane(tx, row, 24) for row in x_rows]
-        )
-
-    right = planes(19, 18, 17, (19, 18, 17))
-    left = planes(8, 9, 10, (8, 9))
-    weights = [read_plane(basis, row, 8) for row in (2, 0, 1)]
-    send_both(pay_a, pay_b, tail_a, tail_b, right + weights[:2], left + weights)
-
-
-def prepare(rhs, accum, trans_x, trans_y, trans_z, center, first_side):
+    def planes(rows, x_rows):
+        near, second, far = rows
+        r, d = read_plane(raw, near), read_plane(dg_n, near)
+        found = [r, low_part(r), read_plane(raw, second)]
+        found += [d, low_part(d), read_plane(dg_n, second)]
+        found += [read_plane(ref, row) for ref in (ty_n, tz_n) for row in (near, second)]
+        found += [first_sweep(far)]
+        found += [read_plane(tx_n, row) for row in x_rows]
+        found += [read_plane(w, near) for w in weights]
+        return found
+
+    right, left = LAST, HEAD
+    send_both(pay_a, pay_b, tail_a, tail_b, planes(right, right), planes(left, left))
+
+
+def prepare(*fields):
     return pl.pallas_call(
         prepare_kernel,
-        out_shape=(payload(),) * 2,
-        in_specs=in_hbm(6) + in_vmem(1),
-        out_specs=tuple(in_vmem(2)),
-        scratch_shapes=[cells(F32)]
-        + [cells()] * 4
-        + [vmem((16, PLANE), BF16)]
-        + [vmem((TILES * 24, LANES))] * 5
-        + [vmem((TILES * 8, LANES))]
-        + tails()
-        + [semaphores(6, PAIRS)],
-        compiler_params=params(58),
-    )(rhs, accum, trans_x, trans_y, trans_z, center, first_side)
+        out_shape=(padded(),) * 8 + (payload(FIRST),) * 2,
+        in_specs=in_hbm(7),
+        out_specs=tuple(in_vmem(10)),
+        scratch_shapes=[cells(F32)] + [cells()] * 7 + tails(FIRST) + [semaphores(8, PAIRS)],
+        compiler_params=params(46),
+        cost_estimate=lasting(6),
+    )(*fields)
 
 
 def add_share(shares, u, v, value):
@@ -334,14 +344,13 @@
 
 
 def presmooth_kernel(
-    got_a, got_b, raw, tx_in, ty_in, tz_in, dg_in, w0, w1, w2, operator,
-    tx, ty, tz, dg, tx_out, ty_out, tz_out, k_out, b_out, smooth_out, w0_out, w1_out, w2_out,
-    part, pay_a, pay_b,
-    k, b, smooth, work, sums, rest, edges, tail_a, tail_b, out_sems,
+    got_a, got_b, raw, tx_in, ty_in, tz_in, dg_in, w0_in, w1_in, w2_in, after,
+    tx, ty, tz, dg, w0, w1, w2,
+    k, b, smooth, edges, pay_a, pay_b,
+    work, tail_a, tail_b, second_a, second_b,
 ):
     weights = (w0, w1, w2)
-    sent = copies(weights, (w0_out, w1_out, w2_out), out_sems.at[0:3])
-    both = received(got_a, got_b, tail_a, tail_b)
+    both = received(FIRST, got_a, got_b, tail_a, tail_b)
     for q in range(WHOLE + 1):
         size = 16 if q < WHOLE else REST
 
@@ -351,9 +360,9 @@
         def get(ref, row):
             return ref[plane(ref, row, q, size), :]
 
-        values = [both(n, q) for n in range(PLANES)]
+        values = [both(n, q) for n in range(FIRST)]
         left, right = [v[0] for v in values], [v[1] for v in values]
-        for got, rows in ((left, (7, 6, 5)), (right, (28, 29, 30))):
+        for got, rows in ((left, BEFORE), (right, BEYOND)):
             put(b, rows[0], got[0] + got[1])
             put(b, rows[1], got[2])
             put(dg, rows[1], got[5])
@@ -364,26 +373,26 @@
             put(b, rows[2], got[10])
             put(tx, rows[0], got[11])
             put(tx, rows[1], got[12])
-        put(tx, 5, left[13])
+            for a, w in enumerate(weights):
+                put(w, rows[0], got[14 + a])
+        put(tx, BEFORE[2], left[13])
         tx_before = left[11]
         tx_last = get(tx, TOP + OWN - 1)
         beyond = right[3] + right[4]
-        put(dg, 7, left[3] + left[4])
-        put(dg, 28, jnp.where(beyond > 0.0, beyond + tx_last, 0.0))
+        put(dg, BEFORE[0], left[3] + left[4])
+        put(dg, BEYOND[0], jnp.where(beyond > 0.0, beyond + tx_last, 0.0))
         put(dg, TOP, get(dg, TOP) + tx_before)
         first = [get(w, TOP) for w in weights]
         last = [get(w, TOP + OWN - 1) for w in weights]
-        from_next = [right[13], right[14], right[15]]
+        from_next = [right[14 + a] for a in range(3)]
         products = [tx_last * last[a] * from_next[c] for a in range(3) for c in range(3)]
         products += [tx_before * first[a] * first[c] for a, c in PAIRED]
         for n, value in enumerate(products):
             edges[plane(edges, n, q, size, 16), :] = value
         edges[plane(edges, 15, q, size, 16), :] = tx_last * 0.0
 
-    sent += copies((tx, ty, tz), (tx_out, ty_out, tz_out), out_sems.at[3:6])
-
     def scale(t, i, carry):
-        here = span(t, 6, 24)
+        here = span(t, TOP - 2, OWN + 4)
         diag = dg[here, :]
         value = jnp.where(diag > 0.0, OMEGA_FINE / diag, 0.0)
         k[here, :] = value
@@ -392,19 +401,34 @@
         return carry
 
     over_tiles(scale, 0)
-    sent += copies((k, b), (k_out, b_out), out_sems.at[6:8])
-    sweep(b, work, tx, ty, tz, k, b, 6, 24)
-    sweep(work, smooth, tx, ty, tz, k, b, 7, 22)
-    sent += copies((smooth,), (smooth_out,), out_sems.at[8:9])
-    planes_r, planes_l = [], []
-    for planes, rows in ((planes_r, (19, 18, 17)), (planes_l, (0, 1, 2))):
-        for row in rows:
-            f = read_plane(smooth, TOP + row)
-            planes += [f, (lambda f: lambda q, size: remainder(f(q, size)))(f)]
-        planes += [read_plane(w, TOP + row) for w in weights for row in rows]
-        planes += [planes[-1]]
-    send_both(pay_a, pay_b, tail_a, tail_b, planes_r, planes_l)
-
+    sweep(b, work, tx, ty, tz, k, b, TOP - 2, OWN + 4)
+    sweep(work, smooth, tx, ty, tz, k, b, TOP - 1, OWN + 2)
+
+    def planes(rows):
+        near = read_plane(smooth, rows[0])
+        found = [near, low_part(near), read_plane(smooth, rows[1]), read_plane(smooth, rows[2])]
+        return found + [read_plane(w, row) for w in weights for row in rows[1:]]
+
+    send_both(pay_a, pay_b, second_a, second_b, planes(LAST), planes(HEAD))
+
+
+def presmooth(got_a, got_b, raw, tx, ty, tz, dg, w0, w1, w2, operator):
+    return pl.pallas_call(
+        presmooth_kernel,
+        out_shape=(padded(),) * 10 + (vmem((TILES * 16, LANES)),) + (payload(SECOND),) * 2,
+        in_specs=in_vmem(11),
+        out_specs=tuple(in_vmem(13)),
+        input_output_aliases={n + 3: n for n in range(7)},
+        scratch_shapes=[padded()] + tails(FIRST) + tails(SECOND),
+        compiler_params=params(8),
+        cost_estimate=lasting(6),
+    )(got_a, got_b, raw, tx, ty, tz, dg, w0, w1, w2, operator)
+
+
+def restrict_kernel(
+    smooth, raw, tx, ty, tz, dg, w0, w1, w2, edges, operator, part, sums, rest
+):
+    weights = (w0, w1, w2)
     sums[...] = jnp.zeros_like(sums)
     lane = lanes_of(64)
     row8 = rows_of(8)
@@ -421,7 +445,7 @@
         for w in weights:
             f = w[span(t, TOP, 24), :] * left_over
             mixed = jnp.where(row8 < BLK - 8, f[8:16], 0.0)
-            folded += [f[0:8] + mixed, f[16:24] + (f[8:16] - mixed)]
+            folded += [f[0:8] + mixed, jnp.where(row8 < 4, f[16:24], 0.0) + (f[8:16] - mixed)]
         folded = jnp.concatenate(folded + [edges[pl.ds(t * 16, 16), :]], axis=0)
         n = t // PAIR
         phase = i % PHASES
@@ -459,33 +483,18 @@
             row = RHS_ROW + 1 + block + OFFSET[a]
             low = (2 * a + block) * 8
             part[row : row + 1, :] += jnp.sum(placed[low : low + 8], axis=0, keepdims=True)
-    for n in range(1, part.shape[0] // ALL_ROWS):
-        part[n * ALL_ROWS : n * ALL_ROWS + ALL_ROWS, :] = part[0:ALL_ROWS, :]
-    for copy in sent:
-        copy.wait()
-
-
-def presmooth(count, got_a, got_b, raw, tx, ty, tz, dg, w0, w1, w2, operator):
-    results = pl.pallas_call(
-        presmooth_kernel,
-        out_shape=(padded(),) * 4
-        + (padded_out(),) * 9
-        + (jax.ShapeDtypeStruct((count * ALL_ROWS, LANES), F32),)
-        + (payload(),) * 2,
+
+
+def restrict(smooth, raw, tx, ty, tz, dg, w0, w1, w2, edges, operator):
+    return pl.pallas_call(
+        restrict_kernel,
+        out_shape=vmem((ALL_ROWS, LANES)),
         in_specs=in_vmem(11),
-        out_specs=tuple(in_vmem(4) + in_hbm(9) + in_vmem(3)),
-        input_output_aliases={3: 0, 4: 1, 5: 2, 6: 3},
-        scratch_shapes=[padded()] * 4
-        + [
-            vmem((PHASES, NCY, 64, LANES)),
-            vmem((PAIR * 24, LANES)),
-            vmem((TILES * 16, LANES)),
-        ]
-        + tails()
-        + [semaphores(9)],
-        compiler_params=params(16),
-    )(got_a, got_b, raw, tx, ty, tz, dg, w0, w1, w2, operator)
-    return results[4:]
+        out_specs=in_vmem(1)[0],
+        scratch_shapes=[vmem((PHASES, NCY, 64, LANES)), vmem((PAIR * 24, LANES))],
+        compiler_params=params(6),
+        cost_estimate=lasting(4),
+    )(smooth, raw, tx, ty, tz, dg, w0, w1, w2, edges, operator)
 
 
 def regrouped(ref, dst, shift, index, load):
@@ -525,49 +534,14 @@
         elif value is None:
             value = jnp.zeros((OWN, LANES), F32)
         dst[index, t, 0:OWN, :] = value
-        dst[index, t, OWN:PAD, :] = jnp.zeros((PAD - OWN, LANES), F32)
+        dst[index, t, OWN:SPREAD, :] = jnp.zeros((SPREAD - OWN, LANES), F32)
 
 
 def assemble_kernel(
-    rhs_in, accum_in, x_in, y_in, z_in, center_in, lower_in, upper_in, inverse, before,
-    out, raw, tx_n, ty_n, tz_n, dg_n, w0_n, w1_n, w2_n,
-    rhs_v, accum_v, x_v, y_v, z_v, center_v, lower_v, upper_v,
-    w, tx, ty, tz, dg, fields, rows_in, found, sems,
+    tx_n, ty_n, tz_n, dg_n, w0_n, w1_n, w2_n, inverse, out,
+    w, tx, ty, tz, dg, fields, rows_in, found,
 ):
-    wait = stream(
-        (rhs_in, accum_in, x_in, y_in, z_in, center_in, lower_in, upper_in),
-        (rhs_v, accum_v, x_v, y_v, z_v, center_v, lower_v, upper_v),
-        sems,
-    )
     weights = (w0_n, w1_n, w2_n)
-    lane = lanes_of(OWN)
-
-    def load(t, i, carry):
-        z_before, y_before, y_second = carry
-        for ref, src in zip(weights, (center_v, lower_v, upper_v)):
-            ref[span(t, TOP, OWN), :] = own(src, t)
-            ref[span(t, TOP + OWN, 4), :] = jnp.zeros((4, LANES), F32)
-        z_pos = (i * LANES + lane) % NZ
-        cells = t * LANES + lane
-        here = span(t, TOP, OWN)
-        x, y, z = own(x_v, t), own(y_v, t), own(z_v, t)
-        y_inner = jnp.where(cells < PLANE - NZ, y, 0.0)
-        z_inner = jnp.where(z_pos != NZ - 1, z, 0.0)
-        z_rolled = lane_roll(z_inner, 1)
-        y_rolled = lane_roll(y_inner, NZ - LANES)
-        tx_n[span(t, 0, TOP), :] = jnp.zeros((TOP, LANES), F32)
-        tx_n[here, :] = x
-        ty_n[here, :] = y_inner
-        tz_n[here, :] = z_inner
-        total = own(accum_v, t) + x + tx_n[span(t, TOP - 1, OWN), :]
-        total = total + y + jnp.where(lane < NZ - LANES, y_second, y_before)
-        total = total + z + jnp.where(lane == 0, z_before, z_rolled)
-        dg_n[here, :] = total
-        raw[here, :] = rhs_v[:, at(t)]
-        return z_rolled, y_rolled, y_before
-
-    zero = lanes_of(OWN).astype(F32) * 0.0
-    over_tiles(load, (zero, zero, zero), wait)
 
     def plain(ref, tile):
         return ref[tile * PAD + TOP : tile * PAD + TOP + OWN, :]
@@ -718,16 +692,14 @@
     out[INVERSE_ROW : INVERSE_ROW + 2, :] = inverse[...]
 
 
-def assemble(rhs, accum, trans_x, trans_y, trans_z, center, lower, upper, inverse, before):
-    slab = (LT, PAD, LANES)
+def assemble(tx, ty, tz, dg, w0, w1, w2, inverse):
+    slab = (LT, SPREAD, LANES)
     return pl.pallas_call(
         assemble_kernel,
-        out_shape=(vmem((ALL_ROWS, LANES)),) + (padded(),) * 8,
-        in_specs=in_hbm(8) + in_vmem(1) + [pl.BlockSpec(memory_space=pl.ANY)],
-        out_specs=tuple(in_vmem(9)),
-        scratch_shapes=[cells(F32)]
-        + [cells()] * 7
-        + [
+        out_shape=vmem((ALL_ROWS, LANES)),
+        in_specs=in_vmem(8),
+        out_specs=in_vmem(1)[0],
+        scratch_shapes=[
             vmem((3, GROUP + 1) + slab),
             vmem((GROUP,) + slab),
             vmem((GROUP,) + slab),
@@ -736,20 +708,25 @@
             vmem((33, 2, LT, 24, LANES)),
             vmem((LT, 456, 2 * LANES)),
             vmem((57, 2 * LANES)),
-            semaphores(8, PAIRS),
         ],
-        compiler_params=params(32),
-    )(rhs, accum, trans_x, trans_y, trans_z, center, lower, upper, inverse, before)
+        compiler_params=params(24),
+        cost_estimate=lasting(10),
+    )(tx, ty, tz, dg, w0, w1, w2, inverse)
 
 
 EDGE = 8
 
 
-def coarse_solve(count, gathered, same, same_t, y_mat, y_mat_t, z_mat, z_mat_t, inv, rhs, e, e_y, e_z):
+def coarse_solve(count, halves_in, gathered, same, same_t, y_mat, y_mat_t, z_mat, z_mat_t, inv, rhs, e, e_y, e_z):
     rows = 2 * count
     here = pl.ds(EDGE, rows)
     for ref in (same, y_mat, z_mat, inv, rhs, e, e_y, e_z):
         ref[...] = jnp.zeros_like(ref)
+    index = lax.axis_index("gx")
+    for n, distance in enumerate(arrival(count)):
+        ref, n = halves_in[n // (count // 2)], n % (count // 2)
+        place = pl.multiple_of(lax.bitwise_xor(index, distance) * ALL_ROWS, ALL_ROWS)
+        gathered[pl.ds(place, ALL_ROWS), :] = ref[n * ALL_ROWS : n * ALL_ROWS + ALL_ROWS, :]
 
     def share(row):
         return gathered[pl.ds(row, count, ALL_ROWS), :]
@@ -799,25 +776,19 @@
 
 
 def finish_kernel(
-    count, gathered_rows, got_a, got_b, smooth_in, tx_in, ty_in, tz_in, k_in, b_in, w0_in, w1_in, w2_in,
-    out, update,
-    smooth, tx, ty, tz, k, b, w0, w1, w2,
-    same, same_t, y_mat, y_mat_t, z_mat, z_mat_t, inv, rhs, e, e_y, e_z, strips, spread, first, second, tail_a, tail_b, sems,
+    count, near_rows, far_rows, got_a, got_b, smooth_in, w0_in, w1_in, w2_in, tx, ty, tz, k, b,
+    out, update, smooth, w0, w1, w2,
+    gathered, same, same_t, y_mat, y_mat_t, z_mat, z_mat_t, inv, rhs, e, e_y, e_z, strips, spread, first, second, tail_a, tail_b,
 ):
     weights = (w0, w1, w2)
-    coming = copies(
-        (smooth_in, w0_in, w1_in, w2_in, tx_in, ty_in, tz_in, k_in, b_in),
-        (smooth, w0, w1, w2, tx, ty, tz, k, b),
-        sems,
-    )
     coarse_solve(
-        count, gathered_rows, same, same_t, y_mat, y_mat_t, z_mat, z_mat_t, inv, rhs, e, e_y, e_z
+        count, (near_rows, far_rows), gathered, same, same_t, y_mat, y_mat_t, z_mat, z_mat_t, inv, rhs, e, e_y, e_z
     )
     base = EDGE + 2 * lax.axis_index("gx")
     update[...] = e[pl.ds(base, 2), :]
     near = {s: e[pl.ds(base + s, 1), :] for s in range(-2, 4)}
-    row = rows_of(PAD)
-    lane = lanes_of(PAD)
+    row = rows_of(SPREAD)
+    lane = lanes_of(SPREAD)
     for a, s in enumerate((0, -1, 1)):
         value = jnp.where(row < TOP + BLK, near[s], near[s + 1])
         value = jnp.where(row < TOP, near[s - 1], value)
@@ -834,24 +805,23 @@
             strips[a, strip] = turned.astype(BF16)
     src = lax.broadcasted_iota(jnp.int32, (LANES, LANES), 0)
     dst = lax.broadcasted_iota(jnp.int32, (LANES, LANES), 1)
-    flat = strips[...].reshape(3 * NCY * PAD, LANES)
+    flat = strips[...].reshape(3 * NCY * SPREAD, LANES)
     for phase in range(PHASES):
         pick = jnp.where((phase * LANES + dst) % NZ // BLK == src % NCZ, 1.0, 0.0).astype(BF16)
         got = jnp.dot(flat, pick, preferred_element_type=F32)
-        spread[phase] = got.reshape(3, NCY, PAD, LANES)
-
-    for copy in coming:
-        copy.wait()
-    both = received(got_a, got_b, tail_a, tail_b)
+        spread[phase] = got.reshape(3, NCY, SPREAD, LANES)
+
+    both = received(SECOND, got_a, got_b, tail_a, tail_b)
     for q in range(WHOLE + 1):
         size = 16 if q < WHOLE else REST
-        values = [both(n, q) for n in range(PLANES)]
-        for side, rows in ((0, (7, 6, 5)), (1, (28, 29, 30))):
+        values = [both(n, q) for n in range(SECOND)]
+        for side, rows in ((0, BEFORE), (1, BEYOND)):
             got = [v[side] for v in values]
-            for n, row in enumerate(rows):
-                smooth[plane(smooth, row, q, size), :] = got[2 * n] + got[2 * n + 1]
-                for a, w in enumerate(weights):
-                    w[plane(w, row, q, size), :] = got[6 + 3 * a + n]
+            for row, value in zip(rows, (got[0] + got[1], got[2], got[3])):
+                smooth[plane(smooth, row, q, size), :] = value
+            for a, w in enumerate(weights):
+                for n, row in enumerate(rows[1:]):
+                    w[plane(w, row, q, size), :] = got[4 + 2 * a + n]
 
     def prolong(t, i, carry):
         n = t // PAIR
@@ -861,17 +831,19 @@
         for a, w in enumerate(weights):
             if i == PAIR // 2:
                 values = jnp.where(
-                    lane < LANES // 2, spread[phase, a, 2 * n], spread[phase, a, 2 * n + 1]
+                    lane[0:PAD] < LANES // 2,
+                    spread[phase, a, 2 * n, 0:PAD],
+                    spread[phase, a, 2 * n + 1, 0:PAD],
                 )
             else:
-                values = spread[phase, a, 2 * n + (1 if i > PAIR // 2 else 0)]
+                values = spread[phase, a, 2 * n + (1 if i > PAIR // 2 else 0), 0:PAD]
             total = total + w[here, :] * values
         first[here, :] = total
         return carry
 
     over_tiles(prolong, 0)
-    sweep(first, second, tx, ty, tz, k, b, 6, 24)
-    sweep(second, first, tx, ty, tz, k, b, 7, 22)
+    sweep(first, second, tx, ty, tz, k, b, TOP - 2, OWN + 4)
+    sweep(second, first, tx, ty, tz, k, b, TOP - 1, OWN + 2)
 
     def last(t, i, carry):
         total, after = coupled(first, tx, ty, tz, t, TOP, OWN, carry)
@@ -882,8 +854,7 @@
     over_tiles(last, coupled_start(first, TOP, OWN))
 
 
-def finish(gathered_rows, got_a, got_b, smooth, tx, ty, tz, k, b, w0, w1, w2):
-    count = gathered_rows.shape[0] // ALL_ROWS
+def finish(count, near_rows, far_rows, got_a, got_b, smooth, w0, w1, w2, tx, ty, tz, k, b):
     rows = 2 * count
 
     def kernel(*refs):
@@ -894,10 +865,12 @@
         out_shape=(
             jax.ShapeDtypeStruct((OWN, PLANE), F32),
             jax.ShapeDtypeStruct((2, LANES), F32),
-        ),
-        in_specs=in_vmem(3) + in_hbm(9),
-        out_specs=tuple(in_vmem(2)),
-        scratch_shapes=[padded()] * 9
+        )
+        + (padded(),) * 4,
+        in_specs=in_vmem(13),
+        out_specs=tuple(in_vmem(6)),
+        input_output_aliases={n + 4: n + 2 for n in range(4)},
+        scratch_shapes=[vmem((count * ALL_ROWS, LANES))]
         + [
             vmem((4, rows + 2 * EDGE, LANES)),
             vmem((3, rows, LANES)),
@@ -908,15 +881,15 @@
         ]
         + [vmem((rows + 2 * EDGE, LANES))] * 5
         + [
-            vmem((3, NCY, PAD, LANES), BF16),
-            vmem((PHASES, 3, NCY, PAD, LANES)),
-            vmem((TILES * PAD, LANES)),
-            vmem((TILES * PAD, LANES)),
+            vmem((3, NCY, SPREAD, LANES), BF16),
+            vmem((PHASES, 3, NCY, SPREAD, LANES)),
+            padded(),
+            padded(),
         ]
-        + tails()
-        + [semaphores(9)],
-        compiler_params=params(58),
-    )(gathered_rows, got_a, got_b, smooth, tx, ty, tz, k, b, w0, w1, w2)
+        + tails(SECOND),
+        compiler_params=params(10 + count // 8),
+        cost_estimate=lasting(12),
+    )(near_rows, far_rows, got_a, got_b, smooth, w0, w1, w2, tx, ty, tz, k, b)[:2]
 
 
 def swapped(pay_a, pay_b):
@@ -926,30 +899,71 @@
     return got_a, lax.ppermute(pay_b, "gx", inner)
 
 
-def spread_out(rows):
+def rounds(count):
+    bits = count.bit_length() - 1
+    found = []
+    while bits >= 4:
+        low = 1 << (bits - 2)
+        found.append((low, 2 * low, 3 * low))
+        bits -= 2
+    return found + [(1 << bit,) for bit in reversed(range(bits))]
+
+
+def arrival(count):
+    order = [0]
+    for steps in rounds(count):
+        order = [distance ^ step for step in (0, *steps) for distance in order]
+    return order
+
+
+def stacked_kernel(*refs):
+    out, low = refs[-1], 0
+    for ref in refs[:-1]:
+        out[low : low + ref.shape[0], :] = ref[...]
+        low += ref.shape[0]
+
+
+def stacked(blocks):
+    rows = sum(block.shape[0] for block in blocks)
+    return pl.pallas_call(
+        stacked_kernel,
+        out_shape=vmem((rows, LANES)),
+        in_specs=in_vmem(len(blocks)),
+        out_specs=in_vmem(1)[0],
+        compiler_params=params(4),
+    )(*blocks)
+
+
+def gather(rows):
     count = lax.axis_size("gx")
-    each = rows.shape[0] // count
-    got = lax.all_to_all(rows.reshape(count, each, LANES), "gx", 0, 0)
-    return got.reshape(count * each, LANES)
+    for steps in rounds(count):
+        blocks = [rows]
+        for step in steps:
+            blocks.append(lax.ppermute(rows, "gx", [(i, i ^ step) for i in range(count)]))
+        if steps != (1,):
+            rows = stacked(blocks)
+    return blocks
 
 
 def per_device(
     rhs, accumulation, trans_x, trans_y, trans_z, basis_center, basis_side, coarse_inverse
 ):
     count = lax.axis_size("gx")
-    pay_a, pay_b = prepare(
-        rhs, accumulation, trans_x, trans_y, trans_z, basis_center, basis_side[:, 0]
+    raw, *own_fields, pay_a, pay_b = prepare(
+        rhs, accumulation, trans_x, trans_y, trans_z, basis_center, basis_side
     )
     got_a, got_b = swapped(pay_a, pay_b)
-    operator, *own_fields = assemble(
-        rhs, accumulation, trans_x, trans_y, trans_z, basis_center, basis_side[0], basis_side[1],
-        coarse_inverse, pay_b,
+    operator = assemble(*own_fields, coarse_inverse)
+    *own_fields, k, b, smooth, edges, pay_a, pay_b = presmooth(
+        got_a, got_b, raw, *own_fields, operator
     )
-    *kept, part, pay_a, pay_b = presmooth(count, got_a, got_b, *own_fields, operator)
     got_a, got_b = swapped(pay_a, pay_b)
-    gathered = spread_out(part)
-    tx, ty, tz, k, b, smooth, w0, w1, w2 = kept
-    return finish(gathered, got_a, got_b, smooth, tx, ty, tz, k, b, w0, w1, w2)
+    part = restrict(smooth, raw, *own_fields, edges, operator)
+    near_rows, far_rows = gather(part)
+    tx, ty, tz, dg, w0, w1, w2 = own_fields
+    return finish(
+        count, near_rows, far_rows, got_a, got_b, smooth, w0, w1, w2, tx, ty, tz, k, b
+    )
 
 
 def solution(mesh):

time: 75.2 us -> 56.1 us (0.75)
  the two profiles are of different devices: /device:TPU:9 before, /device:TPU:11 now
where the time goes in v1:
time: 56.1 us; the launch traced here: 56 us
  Pallas kernels  29.2 us (52%)
  starting transfers between devices  13.6 us (24%)
  waiting for transfers between devices  10.2 us (18%)
  local copies, waits for them, and re-layouts  2.37 us (4%)
  between operations  0.72 us (1%)
    pallas_call x1, Pallas kernels, assemble(): pl.pallas_call(assemble_kernel, out_shape=vmem((ALL_ROWS, LANES)), in_spe...  10.1 us
    ppermute x2, waiting for transfers between devices, swapped(): return (got_a, lax.ppermute(pay_b, 'gx', inner))  8.02 us
    pallas_call x1, Pallas kernels, finish(): pl.pallas_call(kernel, out_shape=(jax.ShapeDtypeStruct((OWN, PLANE), F32)...  7.77 us
    ppermute x2, starting transfers between devices, swapped(): return (got_a, lax.ppermute(pay_b, 'gx', inner))  5.13 us
    ppermute x5, starting transfers between devices, gather(): lax.ppermute(rows, 'gx', [(i, i ^ step) for i in range(count)])  5.13 us
    pallas_call x1, Pallas kernels, prepare(): pl.pallas_call(prepare_kernel, out_shape=(padded(),) * 8 + (payload(FIRST...  4.3 us
    pallas_call x1, Pallas kernels, presmooth(): pl.pallas_call(presmooth_kernel, out_shape=(padded(),) * 10 + (vmem((TILE...  3.83 us
    ppermute x2, starting transfers between devices, swapped(): got_a = lax.ppermute(pay_a, 'gx', [(i, i ^ 1) for i in range(count)])  3.3 us
  transfers between devices with their start and end apart: 9, of which 4 were waited for; matrix products, arithmetic and copies ran while one was open for 0% of the time, Pallas kernels for 18%

profile of v1, /device:TPU:11, one launch (start us, length us, event | category | flops | bytes accessed | tf_op | source)
XLA Modules:
  0.0 56.0 jit_solution(17539763047139338056)
XLA Ops:
  0.6 2.4 %copy.21.side_in = bf16[2,20,12800]{2,1,0:T(8,128)(2,1)} copy(bf16[2,20,12800]{2,0,1:T(2,128)(2,1)} %param.14) | data formatting | bytes 2048000 | tf_op args[6]
  3.0 0.0 copy-start
  3.0 4.3 %shard_map.95 = (f32[2608,128]{1,0:T(8,128)S(1)}, f32[2608,128]{1,0:T(8,128)S(1)}, f32[2608,128]{1,0:T(8,128)S(1)}, f32[2608,128]{1,0:T(8,128)S(1)}, f32[2608,12...) custom-call(f32[20,12800]{1,0:T(8,128)} %rhs_in.1, ...), custom_call_target="tpu_custom_call" | custom-call | bytes 21000000 | tf_op jit(solution)/shard_map/pallas_call | solution.py:326
  7.3 0.7 %collective-permute-start = (bf16[1712,128]{1,0:T(8,128)(2,1)}, bf16[1712,128]{1,0:T(8,128)(2,1)S(1)}, u32[]{:S(2)}, u32[]{:S(2)}) collective-permute-start(bf16[1712,128]{1,0:T(8,128)(2,1)} %get-tuple-element.27), channel_id=1, source_target_pairs={{0,1},{1,0},{2,3},{3,2},{4,5},{5,4},{6,7},{7,6},{8,9},{9,8},{10,11... | collective-permute-start | bytes 1314824 | tf_op jit(solution)/shard_map/ppermute | solution.py:897
  8.0 3.0 %collective-permute-start.1 = (bf16[1712,128]{1,0:T(8,128)(2,1)}, bf16[1712,128]{1,0:T(8,128)(2,1)S(1)}, u32[]{:S(2)}, u32[]{:S(2)}) collective-permute-start(bf16[1712,128]{1,0:T(8,128)(2,1)} %get-tuple-element.28), channel_id=1, source_target_pairs={{1,2},{2,1},{3,4},{4,3},{5,6},{6,5},{7,8},{8,7},{9,10},{10,9},{11,... | collective-permute-start | bytes 1314824 | tf_op jit(solution)/shard_map/ppermute | solution.py:899
  11.1 0.0 copy-done
  11.1 10.1 %shard_map.96.after.operator = f32[48,128]{1,0:T(8,128)S(1)} custom-call(f32[2608,128]{1,0:T(8,128)S(1)} %get-tuple-element.30.tx_n.tx_in, f32[2608,128]{1,0:T(8,128)S(1)} %get-tuple-element.31.ty_n.ty_in, f32[2608,128]{1,0:T(8,128)S(1)} %get-tuple-element.32.tz_n.tz_in, f32[2608,128]{1,0:T(8,128)S(1)} %get-tuple-element.33.dg_n.dg_in, ...), custom_call_target="tpu_custom_call" | custom-call | bytes 35000000 | tf_op jit(solution)/shard_map/pallas_call | solution.py:697
  21.3 0.0 collective-permute-done.got_a
  21.3 1.3 %collective-permute-done.1.got_b = bf16[1712,128]{1,0:T(8,128)(2,1)S(1)} collective-permute-done((bf16[1712,128]{1,0:T(8,128)(2,1)}, bf16[1712,128]{1,0:T(8,128)(2,1)S(1)}, u32[]{:S(2)}, u32[]{:S(2)}) %collective-permute-start.1) | collective-permute-done | bytes 438304 | tf_op jit(solution)/shard_map/ppermute | solution.py:899
  22.5 3.8 %shard_map.97 = (f32[2608,128]{1,0:T(8,128)S(1)}, f32[2608,128]{1,0:T(8,128)S(1)}, f32[2608,128]{1,0:T(8,128)S(1)}, f32[2608,128]{1,0:T(8,128)S(1)}, f32[2608,12...) custom-call(bf16[1712,128]{1,0:T(8,128)(2,1)S(1)} %collective-permut, ...), custom_call_target="tpu_custom_call", output_to_operand_aliasing={{0}: (3, {}), {1}: (4, {}), {2}: (5, {}), {3}: (6, {}), {4}... | custom-call | bytes 21000000 | tf_op jit(solution)/shard_map/pallas_call | solution.py:416
  26.4 3.1 %shard_map.98.refs_0_ = f32[48,128]{1,0:T(8,128)S(1)} custom-call(f32[2608,128]{1,0:T(8,128)S(1)} %get-tuple-element.37.smooth.refs_4_, f32[2608,128]{1,0:T(8,128)S(1)} %get-tuple-element.29.raw, f32[2608,128]{1,0:T(8,128)S(1)} %get-tuple-element.38.tx.refs_8_, f32[2608,128]{1,0:T(8,128)S(1)} %get-tuple-element.39.ty.refs_9_, ...), custom_call_target="tpu_custom_call" | custom-call | bytes 14000000 | tf_op jit(solution)/shard_map/pallas_call | solution.py:489
  29.5 1.4 %collective-permute-start.4 = (f32[48,128]{1,0:T(8,128)S(1)}, f32[48,128]{1,0:T(8,128)S(1)}, u32[]{:S(2)}, u32[]{:S(2)}) collective-permute-start(f32[48,128]{1,0:T(8,128)S(1)} %shard_map.98.refs_0_), channel_id=1, source_target_pairs={{0,12},{1,13},{2,14},{3,15},{4,8},{5,9},{6,10},{7,11},{8,4},{9,5},... | collective-permute-start | bytes 73736 | tf_op jit(solution)/shard_map/ppermute | solution.py:942
  30.8 1.1 %collective-permute-start.3 = (f32[48,128]{1,0:T(8,128)S(1)}, f32[48,128]{1,0:T(8,128)S(1)}, u32[]{:S(2)}, u32[]{:S(2)}) collective-permute-start(f32[48,128]{1,0:T(8,128)S(1)} %shard_map.98.refs_0_), channel_id=1, source_target_pairs={{0,8},{1,9},{2,10},{3,11},{4,12},{5,13},{6,14},{7,15},{8,0},{9,1},... | collective-permute-start | bytes 73736 | tf_op jit(solution)/shard_map/ppermute | solution.py:942
  31.9 1.1 %collective-permute-start.2 = (f32[48,128]{1,0:T(8,128)S(1)}, f32[48,128]{1,0:T(8,128)S(1)}, u32[]{:S(2)}, u32[]{:S(2)}) collective-permute-start(f32[48,128]{1,0:T(8,128)S(1)} %shard_map.98.refs_0_), channel_id=1, source_target_pairs={{0,4},{1,5},{2,6},{3,7},{4,0},{5,1},{6,2},{7,3},{8,12},{9,13},{10,... | collective-permute-start | bytes 73736 | tf_op jit(solution)/shard_map/ppermute | solution.py:942
  33.0 0.0 collective-permute-done.4.refs_3_
  33.0 1.7 %collective-permute-done.3.refs_2_ = f32[48,128]{1,0:T(8,128)S(1)} collective-permute-done((f32[48,128]{1,0:T(8,128)S(1)}, f32[48,128]{1,0:T(8,128)S(1)}, u32[]{:S(2)}, u32[]{:S(2)}) %collective-permute-start.3) | collective-permute-done | bytes 24608 | tf_op jit(solution)/shard_map/ppermute | solution.py:942
  34.7 0.4 collective-permute-done.2.refs_1_
  35.2 0.1 collective-permute-start.5
  35.2 2.6 %collective-permute-start.7 = (bf16[1008,128]{1,0:T(8,128)(2,1)S(1)}, bf16[1008,128]{1,0:T(8,128)(2,1)S(1)}, u32[]{:S(2)}, u32[]{:S(2)}) collective-permute-start(bf16[1008,128]{1,0:T(8,128)(2,1)S(1)} %get-tuple-element.46), channel_id=1, source_target_pairs={{0,1},{1,0},{2,3},{3,2},{4,5},{5,4},{6,7},{7,6},{8,9},{9,8},{10,11... | collective-permute-start | bytes 774152 | tf_op jit(solution)/shard_map/ppermute | solution.py:897
  37.8 2.1 %collective-permute-start.8 = (bf16[1008,128]{1,0:T(8,128)(2,1)S(1)}, bf16[1008,128]{1,0:T(8,128)(2,1)S(1)}, u32[]{:S(2)}, u32[]{:S(2)}) collective-permute-start(bf16[1008,128]{1,0:T(8,128)(2,1)S(1)} %get-tuple-element.47), channel_id=1, source_target_pairs={{1,2},{2,1},{3,4},{4,3},{5,6},{6,5},{7,8},{8,7},{9,10},{10,9},{11,... | collective-permute-start | bytes 774152 | tf_op jit(solution)/shard_map/ppermute | solution.py:899
  39.9 0.0 collective-permute-done.5.refs_1_
  39.9 1.5 %collective-permute-start.6 = (f32[384,128]{1,0:T(8,128)S(1)}, f32[384,128]{1,0:T(8,128)S(1)}, u32[]{:S(2)}, u32[]{:S(2)}) collective-permute-start(f32[384,128]{1,0:T(8,128)S(1)} %shard_map.100.refs_0_), channel_id=1, source_target_pairs={{0,1},{1,0},{2,3},{3,2},{4,5},{5,4},{6,7},{7,6},{8,9},{9,8},{10,11... | collective-permute-start | bytes 589832 | tf_op jit(solution)/shard_map/ppermute | solution.py:942
  41.4 0.0 collective-permute-done.7.refs_2_
  41.4 6.8 %collective-permute-done.8.refs_3_ = bf16[1008,128]{1,0:T(8,128)(2,1)S(1)} collective-permute-done((bf16[1008,128]{1,0:T(8,128)(2,1)S(1)}, bf16[1008,128]{1,0:T(8,128)(2,1)S(1)}, u32[]{:S(2)}, u32[]{:S(2)}) %collective-permute-start.8) | collective-permute-done | bytes 258080 | tf_op jit(solution)/shard_map/ppermute | solution.py:899
  48.2 0.0 collective-permute-done.6.refs_1_
  48.2 7.8 %shard_map.101 = (f32[20,12800]{1,0:T(8,128)}, f32[2,128]{1,0:T(2,128)}, f32[2608,128]{1,0:T(8,128)S(1)}, f32[2608,128]{1,0:T(8,128)S(1)}, f32[2608,128]{1,0:T(8,128)S(1)}, /*index=5*/f32[2608,128]{1,0:T(8,128)S(1)}) custom-call(f32[384,128]{1,0:T(8,128)S(1)} %shard_map.100.refs_0_, ...), custom_call_target="tpu_custom_call", output_to_operand_aliasing={{2}: (4, {}), {3}: (5, {}), {4}: (6, {}), {5}: (7, {})} | custom-call | bytes 42000000 | tf_op jit(solution)/shard_map/pallas_call | solution.py:863
  (2 shorter events, 0.0 us)
Async XLA Ops:
  3.0 8.1 %copy-start = (f32[2,128]{1,0:T(2,128)S(1)}, f32[2,128]{1,0:T(2,128)}, u32[]{:S(2)}) copy-start(f32[2,128]{1,0:T(2,128)} %inverse.1) | copy-start | bytes 3076
  7.3 13.9 %collective-permute-start = (bf16[1712,128]{1,0:T(8,128)(2,1)}, bf16[1712,128]{1,0:T(8,128)(2,1)S(1)}, u32[]{:S(2)}, u32[]{:S(2)}) collective-permute-start(bf16[1712,128]{1,0:T(8,128)(2,1)} %get-tuple-element.27), channel_id=1, source_target_pairs={{0,1},{1,0},{2,3},{3,2},{4,5},{5,4},{6,7},{7,6},{8,9},{9,8},{10,11... | collective-permute-start | bytes 1314824 | tf_op jit(solution)/shard_map/ppermute | solution.py:897
  8.0 14.5 %collective-permute-start.1 = (bf16[1712,128]{1,0:T(8,128)(2,1)}, bf16[1712,128]{1,0:T(8,128)(2,1)S(1)}, u32[]{:S(2)}, u32[]{:S(2)}) collective-permute-start(bf16[1712,128]{1,0:T(8,128)(2,1)} %get-tuple-element.28), channel_id=1, source_target_pairs={{1,2},{2,1},{3,4},{4,3},{5,6},{6,5},{7,8},{8,7},{9,10},{10,9},{11,... | collective-permute-start | bytes 1314824 | tf_op jit(solution)/shard_map/ppermute | solution.py:899
  29.5 3.6 %collective-permute-start.4 = (f32[48,128]{1,0:T(8,128)S(1)}, f32[48,128]{1,0:T(8,128)S(1)}, u32[]{:S(2)}, u32[]{:S(2)}) collective-permute-start(f32[48,128]{1,0:T(8,128)S(1)} %shard_map.98.refs_0_), channel_id=1, source_target_pairs={{0,12},{1,13},{2,14},{3,15},{4,8},{5,9},{6,10},{7,11},{8,4},{9,5},... | collective-permute-start | bytes 73736 | tf_op jit(solution)/shard_map/ppermute | solution.py:942
  30.8 3.9 %collective-permute-start.3 = (f32[48,128]{1,0:T(8,128)S(1)}, f32[48,128]{1,0:T(8,128)S(1)}, u32[]{:S(2)}, u32[]{:S(2)}) collective-permute-start(f32[48,128]{1,0:T(8,128)S(1)} %shard_map.98.refs_0_), channel_id=1, source_target_pairs={{0,8},{1,9},{2,10},{3,11},{4,12},{5,13},{6,14},{7,15},{8,0},{9,1},... | collective-permute-start | bytes 73736 | tf_op jit(solution)/shard_map/ppermute | solution.py:942
  31.9 3.2 %collective-permute-start.2 = (f32[48,128]{1,0:T(8,128)S(1)}, f32[48,128]{1,0:T(8,128)S(1)}, u32[]{:S(2)}, u32[]{:S(2)}) collective-permute-start(f32[48,128]{1,0:T(8,128)S(1)} %shard_map.98.refs_0_), channel_id=1, source_target_pairs={{0,4},{1,5},{2,6},{3,7},{4,0},{5,1},{6,2},{7,3},{8,12},{9,13},{10,... | collective-permute-start | bytes 73736 | tf_op jit(solution)/shard_map/ppermute | solution.py:942
  35.2 4.7 %collective-permute-start.5 = (f32[192,128]{1,0:T(8,128)S(1)}, f32[192,128]{1,0:T(8,128)S(1)}, u32[]{:S(2)}, u32[]{:S(2)}) collective-permute-start(f32[192,128]{1,0:T(8,128)S(1)} %shard_map.99.refs_0_), channel_id=1, source_target_pairs={{0,2},{1,3},{2,0},{3,1},{4,6},{5,7},{6,4},{7,5},{8,10},{9,11},{10,... | collective-permute-start | bytes 294920 | tf_op jit(solution)/shard_map/ppermute | solution.py:942
  35.2 6.2 %collective-permute-start.7 = (bf16[1008,128]{1,0:T(8,128)(2,1)S(1)}, bf16[1008,128]{1,0:T(8,128)(2,1)S(1)}, u32[]{:S(2)}, u32[]{:S(2)}) collective-permute-start(bf16[1008,128]{1,0:T(8,128)(2,1)S(1)} %get-tuple-element.46), channel_id=1, source_target_pairs={{0,1},{1,0},{2,3},{3,2},{4,5},{5,4},{6,7},{7,6},{8,9},{9,8},{10,11... | collective-permute-start | bytes 774152 | tf_op jit(solution)/shard_map/ppermute | solution.py:897
  37.8 10.4 %collective-permute-start.8 = (bf16[1008,128]{1,0:T(8,128)(2,1)S(1)}, bf16[1008,128]{1,0:T(8,128)(2,1)S(1)}, u32[]{:S(2)}, u32[]{:S(2)}) collective-permute-start(bf16[1008,128]{1,0:T(8,128)(2,1)S(1)} %get-tuple-element.47), channel_id=1, source_target_pairs={{1,2},{2,1},{3,4},{4,3},{5,6},{6,5},{7,8},{8,7},{9,10},{10,9},{11,... | collective-permute-start | bytes 774152 | tf_op jit(solution)/shard_map/ppermute | solution.py:899
  39.9 8.3 %collective-permute-start.6 = (f32[384,128]{1,0:T(8,128)S(1)}, f32[384,128]{1,0:T(8,128)S(1)}, u32[]{:S(2)}, u32[]{:S(2)}) collective-permute-start(f32[384,128]{1,0:T(8,128)S(1)} %shard_map.100.refs_0_), channel_id=1, source_target_pairs={{0,1},{1,0},{2,3},{3,2},{4,5},{5,4},{6,7},{7,6},{8,9},{9,8},{10,11... | collective-permute-start | bytes 589832 | tf_op jit(solution)/shard_map/ppermute | solution.py:942

commit v2 on v1

--- a/solution.py
+++ b/solution.py
@@ -32,8 +32,8 @@
 QUARTERS = 4
 LT = QUARTERS * NZ // LANES
 PAIRED = ((0, 0), (0, 1), (0, 2), (1, 1), (1, 2), (2, 2))
-FIRST = 17
-SECOND = 10
+FIRST = 12
+SECOND = 15
 WHOLE = TILES // 16
 REST = TILES % 16
 OFFSET = (0, -1, 1)
@@ -43,7 +43,8 @@
 Z_ROW = Y_ROW + len(ACROSS)
 INVERSE_ROW = Z_ROW + len(ACROSS)
 RHS_ROW = INVERSE_ROW + 2
-ALL_ROWS = 48
+ALL_ROWS = 56
+EDGES = 24
 F32 = jnp.float32
 BF16 = jnp.bfloat16
 
@@ -151,6 +152,14 @@
     return lax.fori_loop(0, PAIRS, step, carry, unroll=unroll)
 
 
+def z_blocks(phase, lane_side):
+    cell = lax.broadcasted_iota(jnp.int32, (LANES, LANES), lane_side) + phase * LANES % NZ
+    cell = jnp.where(cell >= NZ, cell - NZ, cell)
+    first = lax.broadcasted_iota(jnp.int32, (LANES, LANES), 1 - lane_side)
+    first = (first % NCZ if lane_side else first) * BLK
+    return jnp.where((cell >= first) & (cell < first + BLK), 1.0, 0.0).astype(BF16)
+
+
 def halves(value):
     high = value.astype(BF16)
     low = (value - high.astype(F32)).astype(BF16)
@@ -166,11 +175,12 @@
 
 
 def coupled(src, tx, ty, tz, t, low, count, carry):
-    center, following, y_next, z_flux, y_flux, y_flux_before = carry
+    center, following, turned, y_next, z_flux, y_flux, y_flux_before = carry
     lane = lanes_of(count)
     here = span(t, low, count)
     second = src[span(jnp.minimum(t + 2, TILES - 1), low, count), :]
-    z_up = jnp.where(lane == LANES - 1, lane_roll(following, -1), lane_roll(center, -1))
+    turned_next = lane_roll(following, -1)
+    z_up = jnp.where(lane == LANES - 1, turned_next, turned)
     y_second = lane_roll(second, -(NZ - LANES))
     y_up = jnp.where(lane >= 2 * LANES - NZ, y_second, y_next)
     tz_t = tz[here, :]
@@ -183,14 +193,15 @@
     total = total + (ty_t * y_up + y_down)
     total = total + tx[here, :] * src[span(t, low + 1, count), :]
     total = total + tx[span(t, low - 1, count), :] * src[span(t, low - 1, count), :]
-    return total, (following, second, y_second, z_flux_new, y_flux_new, y_flux)
+    return total, (following, second, turned_next, y_second, z_flux_new, y_flux_new, y_flux)
 
 
 def coupled_start(src, low, count):
     center = src[span(0, low, count), :]
     following = src[span(1, low, count), :]
     zero = center * 0.0
-    return center, following, lane_roll(following, -(NZ - LANES)), zero, zero, zero
+    turned = lane_roll(center, -1)
+    return center, following, turned, lane_roll(following, -(NZ - LANES)), zero, zero, zero
 
 
 def sweep(src, dst, tx, ty, tz, k, b, low, count):
@@ -307,19 +318,16 @@
         r, d = read_plane(raw, row), read_plane(dg_n, row)
         return lambda q, size: OMEGA_FINE * r(q, size) / d(q, size)
 
-    def planes(rows, x_rows):
-        near, second, far = rows
+    def planes(rows):
+        near, second, _ = rows
         r, d = read_plane(raw, near), read_plane(dg_n, near)
-        found = [r, low_part(r), read_plane(raw, second)]
-        found += [d, low_part(d), read_plane(dg_n, second)]
-        found += [read_plane(ref, row) for ref in (ty_n, tz_n) for row in (near, second)]
-        found += [first_sweep(far)]
-        found += [read_plane(tx_n, row) for row in x_rows]
-        found += [read_plane(w, near) for w in weights]
-        return found
+        found = [r, low_part(r), d, low_part(d)]
+        found += [read_plane(ty_n, near), read_plane(tz_n, near), first_sweep(second)]
+        found += [read_plane(tx_n, row) for row in rows[:2]]
+        return found + [read_plane(w, near) for w in weights]
 
     right, left = LAST, HEAD
-    send_both(pay_a, pay_b, tail_a, tail_b, planes(right, right), planes(left, left))
+    send_both(pay_a, pay_b, tail_a, tail_b, planes(right), planes(left))
 
 
 def prepare(*fields):
@@ -344,10 +352,10 @@
 
 
 def presmooth_kernel(
-    got_a, got_b, raw, tx_in, ty_in, tz_in, dg_in, w0_in, w1_in, w2_in, after,
+    got_a, got_b, raw, tx_in, ty_in, tz_in, dg_in, w0_in, w1_in, w2_in, operator,
     tx, ty, tz, dg, w0, w1, w2,
-    k, b, smooth, edges, pay_a, pay_b,
-    work, tail_a, tail_b, second_a, second_b,
+    k, b, smooth, part, pay_a, pay_b,
+    work, tail_a, tail_b, second_a, second_b, edges, sums, rest, shares_v,
 ):
     weights = (w0, w1, w2)
     both = received(FIRST, got_a, got_b, tail_a, tail_b)
@@ -364,35 +372,31 @@
         left, right = [v[0] for v in values], [v[1] for v in values]
         for got, rows in ((left, BEFORE), (right, BEYOND)):
             put(b, rows[0], got[0] + got[1])
-            put(b, rows[1], got[2])
-            put(dg, rows[1], got[5])
-            put(ty, rows[0], got[6])
-            put(ty, rows[1], got[7])
-            put(tz, rows[0], got[8])
-            put(tz, rows[1], got[9])
-            put(b, rows[2], got[10])
-            put(tx, rows[0], got[11])
-            put(tx, rows[1], got[12])
+            put(ty, rows[0], got[4])
+            put(tz, rows[0], got[5])
+            put(b, rows[1], got[6])
+            put(tx, rows[0], got[7])
+            put(tx, rows[1], got[8])
             for a, w in enumerate(weights):
-                put(w, rows[0], got[14 + a])
-        put(tx, BEFORE[2], left[13])
-        tx_before = left[11]
-        tx_last = get(tx, TOP + OWN - 1)
-        beyond = right[3] + right[4]
-        put(dg, BEFORE[0], left[3] + left[4])
+                put(w, rows[0], got[9 + a])
+        tx_before = left[7]
+        tx_last = get(tx, LAST[0])
+        beyond = right[2] + right[3]
+        put(dg, BEFORE[0], left[2] + left[3])
         put(dg, BEYOND[0], jnp.where(beyond > 0.0, beyond + tx_last, 0.0))
-        put(dg, TOP, get(dg, TOP) + tx_before)
-        first = [get(w, TOP) for w in weights]
-        last = [get(w, TOP + OWN - 1) for w in weights]
-        from_next = [right[14 + a] for a in range(3)]
+        put(dg, HEAD[0], get(dg, HEAD[0]) + tx_before)
+        first = [get(w, HEAD[0]) for w in weights]
+        last = [get(w, LAST[0]) for w in weights]
+        from_next = [right[9 + a] for a in range(3)]
         products = [tx_last * last[a] * from_next[c] for a in range(3) for c in range(3)]
         products += [tx_before * first[a] * first[c] for a, c in PAIRED]
         for n, value in enumerate(products):
-            edges[plane(edges, n, q, size, 16), :] = value
-        edges[plane(edges, 15, q, size, 16), :] = tx_last * 0.0
+            edges[plane(edges, n, q, size, EDGES), :] = value
 
     def scale(t, i, carry):
-        here = span(t, TOP - 2, OWN + 4)
+        here = span(t, TOP - 1, OWN + 2)
+        for row in (TOP - 1, TOP + OWN):
+            smooth[span(t, row, 1), :] = jnp.zeros((1, LANES), F32)
         diag = dg[here, :]
         value = jnp.where(diag > 0.0, OMEGA_FINE / diag, 0.0)
         k[here, :] = value
@@ -400,37 +404,30 @@
         b[here, :] = value * b[here, :]
         return carry
 
-    over_tiles(scale, 0)
-    sweep(b, work, tx, ty, tz, k, b, TOP - 2, OWN + 4)
-    sweep(work, smooth, tx, ty, tz, k, b, TOP - 1, OWN + 2)
+    over_tiles(scale, 0, unroll=4)
+    sweep(b, work, tx, ty, tz, k, b, TOP - 1, OWN + 2)
+    sweep(work, smooth, tx, ty, tz, k, b, TOP, OWN)
+    for q in range(WHOLE + 1):
+        size = 16 if q < WHOLE else REST
+        last = tx[plane(tx, LAST[0], q, size), :] * smooth[plane(smooth, LAST[0], q, size), :]
+        first = tx[plane(tx, BEFORE[0], q, size), :] * smooth[plane(smooth, HEAD[0], q, size), :]
+        values = [last * w[plane(w, BEYOND[0], q, size), :] for w in weights]
+        values += [first * w[plane(w, BEFORE[0], q, size), :] for w in weights]
+        values += [jnp.zeros((size, LANES), F32)] * 3
+        for n, value in enumerate(values):
+            edges[plane(edges, 15 + n, q, size, EDGES), :] = value
 
     def planes(rows):
         near = read_plane(smooth, rows[0])
         found = [near, low_part(near), read_plane(smooth, rows[1]), read_plane(smooth, rows[2])]
-        return found + [read_plane(w, row) for w in weights for row in rows[1:]]
+        found += [read_plane(w, row) for w in weights for row in rows[1:]]
+        found += [read_plane(ref, rows[1]) for ref in (raw, dg, ty, tz)]
+        return found + [read_plane(tx, rows[2])]
 
     send_both(pay_a, pay_b, second_a, second_b, planes(LAST), planes(HEAD))
 
-
-def presmooth(got_a, got_b, raw, tx, ty, tz, dg, w0, w1, w2, operator):
-    return pl.pallas_call(
-        presmooth_kernel,
-        out_shape=(padded(),) * 10 + (vmem((TILES * 16, LANES)),) + (payload(SECOND),) * 2,
-        in_specs=in_vmem(11),
-        out_specs=tuple(in_vmem(13)),
-        input_output_aliases={n + 3: n for n in range(7)},
-        scratch_shapes=[padded()] + tails(FIRST) + tails(SECOND),
-        compiler_params=params(8),
-        cost_estimate=lasting(6),
-    )(got_a, got_b, raw, tx, ty, tz, dg, w0, w1, w2, operator)
-
-
-def restrict_kernel(
-    smooth, raw, tx, ty, tz, dg, w0, w1, w2, edges, operator, part, sums, rest
-):
-    weights = (w0, w1, w2)
-    sums[...] = jnp.zeros_like(sums)
-    lane = lanes_of(64)
+    rows = 48 + EDGES
+    lane = lanes_of(rows)
     row8 = rows_of(8)
     for n in range(PAIR):
         rest[n * 24 + 16 : n * 24 + 24, :] = jnp.zeros((8, LANES), F32)
@@ -446,28 +443,41 @@
             f = w[span(t, TOP, 24), :] * left_over
             mixed = jnp.where(row8 < BLK - 8, f[8:16], 0.0)
             folded += [f[0:8] + mixed, jnp.where(row8 < 4, f[16:24], 0.0) + (f[8:16] - mixed)]
-        folded = jnp.concatenate(folded + [edges[pl.ds(t * 16, 16), :]], axis=0)
-        n = t // PAIR
-        phase = i % PHASES
-        if i != PAIR // 2:
-            sums[phase, 2 * n + (1 if i > PAIR // 2 else 0)] += folded
-        else:
-            sums[phase, 2 * n] += jnp.where(lane < LANES // 2, folded, 0.0)
-            sums[phase, 2 * n + 1] += jnp.where(lane < LANES // 2, 0.0, folded)
+        for n, value in enumerate(folded):
+            shares_v[pl.ds(t * rows + 8 * n, 8), :] = value
+        shares_v[pl.ds(t * rows + 48, EDGES), :] = edges[pl.ds(t * EDGES, EDGES), :]
         return following
 
-    over_tiles(residual, coupled_start(smooth, TOP, OWN))
-
-    src = lax.broadcasted_iota(jnp.int32, (LANES, LANES), 0)
-    dst = lax.broadcasted_iota(jnp.int32, (LANES, LANES), 1)
-    found = jnp.zeros((NCY * 64, LANES), F32)
+    over_tiles(residual, coupled_start(smooth, TOP, OWN), unroll=4)
+
+    def strips(n, carry):
+        for strip in range(2):
+            for phase in range(PHASES):
+                total = None
+                for i in range(phase, PAIR, PHASES):
+                    if strip == 0 and i > PAIR // 2 or strip == 1 and i < PAIR // 2:
+                        continue
+                    value = shares_v[pl.ds((n * PAIR + i) * rows, rows), :]
+                    if i == PAIR // 2:
+                        value = jnp.where((lane < LANES // 2) == (strip == 0), value, 0.0)
+                    total = value if total is None else total + value
+                sums[phase, 2 * n + strip] = total
+        return carry
+
+    lax.fori_loop(0, PAIRS, strips, 0)
+
+    found = jnp.zeros((NCY * (48 + EDGES), LANES), F32)
     for phase in range(PHASES):
-        pick = jnp.where((phase * LANES + src) % NZ // BLK == dst, 1.0, 0.0).astype(BF16)
-        for piece in halves(sums[phase].reshape(NCY * 64, LANES)):
-            found = found + jnp.dot(piece, pick, preferred_element_type=F32)
-    placed = found[0:64]
+        pick = z_blocks(phase, 0)
+        pieces = halves(sums[phase].reshape(NCY * (48 + EDGES), LANES))
+        found = found + jnp.dot(
+            jnp.concatenate(pieces, axis=1),
+            jnp.concatenate([pick, pick], axis=0),
+            preferred_element_type=F32,
+        )
+    placed = found[0:rows]
     for strip in range(1, NCY):
-        placed = placed + lane_roll(found[strip * 64 : strip * 64 + 64], strip * NCZ)
+        placed = placed + lane_roll(found[strip * rows : strip * rows + rows], strip * NCZ)
     shares = {}
     for n, (a, c) in enumerate(PAIRED):
         add_share(shares, 1 + OFFSET[a], 1 + OFFSET[c], placed[57 + n : 58 + n])
@@ -480,24 +490,36 @@
             part[n : n + 1, :] += shares[pair]
     for a in range(3):
         for block in range(2):
-            row = RHS_ROW + 1 + block + OFFSET[a]
+            row = RHS_ROW + 2 + block + OFFSET[a]
             low = (2 * a + block) * 8
             part[row : row + 1, :] += jnp.sum(placed[low : low + 8], axis=0, keepdims=True)
-
-
-def restrict(smooth, raw, tx, ty, tz, dg, w0, w1, w2, edges, operator):
+        for low, u in ((63, 3), (66, 0)):
+            row = RHS_ROW + 1 + u + OFFSET[a]
+            part[row : row + 1, :] += placed[low + a : low + a + 1]
+
+
+def presmooth(got_a, got_b, raw, tx, ty, tz, dg, w0, w1, w2, operator):
     return pl.pallas_call(
-        restrict_kernel,
-        out_shape=vmem((ALL_ROWS, LANES)),
+        presmooth_kernel,
+        out_shape=(padded(),) * 10 + (vmem((ALL_ROWS, LANES)),) + (payload(SECOND),) * 2,
         in_specs=in_vmem(11),
-        out_specs=in_vmem(1)[0],
-        scratch_shapes=[vmem((PHASES, NCY, 64, LANES)), vmem((PAIR * 24, LANES))],
-        compiler_params=params(6),
-        cost_estimate=lasting(4),
-    )(smooth, raw, tx, ty, tz, dg, w0, w1, w2, edges, operator)
-
-
-def regrouped(ref, dst, shift, index, load):
+        out_specs=tuple(in_vmem(13)),
+        input_output_aliases={n + 3: n for n in range(7)},
+        scratch_shapes=[padded()]
+        + tails(FIRST)
+        + tails(SECOND)
+        + [
+            vmem((TILES * EDGES, LANES)),
+            vmem((PHASES, NCY, 48 + EDGES, LANES)),
+            vmem((PAIR * 24, LANES)),
+            vmem((TILES * (48 + EDGES), LANES)),
+        ],
+        compiler_params=params(14),
+        cost_estimate=lasting(8),
+    )(got_a, got_b, raw, tx, ty, tz, dg, w0, w1, w2, operator)
+
+
+def regrouped(ref, dst, shift, index, load, cut=False):
     lane = lanes_of(OWN)
     rolled = {}
 
@@ -533,8 +555,13 @@
             value = jnp.where(lane < last * NZ - t * LANES, value, other)
         elif value is None:
             value = jnp.zeros((OWN, LANES), F32)
+        if cut:
+            value = jnp.where(rows_of(OWN) < OWN - 1, value, 0.0)
         dst[index, t, 0:OWN, :] = value
-        dst[index, t, OWN:SPREAD, :] = jnp.zeros((SPREAD - OWN, LANES), F32)
+        if index >= BLK:
+            dst[index - BLK, t, OWN : OWN + 4, :] = value[16:OWN]
+        else:
+            dst[index, t, 24:SPREAD, :] = jnp.zeros((SPREAD - 24, LANES), F32)
 
 
 def assemble_kernel(
@@ -547,7 +574,7 @@
         return ref[tile * PAD + TOP : tile * PAD + TOP + OWN, :]
 
     for g in range(GROUP):
-        regrouped(tx_n, tx, g, g, plain)
+        regrouped(tx_n, tx, g, g, plain, cut=True)
         regrouped(ty_n, ty, g, g, plain)
         regrouped(tz_n, tz, g, g, plain)
         regrouped(dg_n, dg, g, g, plain)
@@ -558,9 +585,10 @@
     lane8 = lanes_of(8)
 
     def combo(index, carry):
-        half = index // (LT * 3)
-        t = (index // 3) % LT
-        low = (index % 3) * 8
+        shared = index >= 4 * LT
+        half = jnp.where(shared, 0, index // (2 * LT))
+        t = jnp.where(shared, index - 4 * LT, index // 2 % LT)
+        low = jnp.where(shared, 16, index % 2 * 8)
         t_next = jnp.minimum(t + 1, LT - 1)
         same = pl.ds(pl.multiple_of(low, 8), 8)
         after = pl.ds(low + 1, 8)
@@ -609,7 +637,7 @@
             fields[15 + n, half, t, same, :] = z_sum[n]
         return carry
 
-    lax.fori_loop(0, 2 * LT * 3, combo, 0)
+    lax.fori_loop(0, 5 * LT, combo, 0)
 
     row8 = rows_of(8)
 
@@ -618,8 +646,11 @@
         t = index % LT
         cols = pl.ds(pl.multiple_of(half * LANES, LANES), LANES)
 
+        mine = (row8 < 4) == (half == 0)
+
         def tiles_of(n):
-            return [fields[n, half, t, 8 * s : 8 * s + 8, :] for s in range(3)]
+            found = [fields[n, half, t, 8 * s : 8 * s + 8, :] for s in range(2)]
+            return found + [jnp.where(mine, fields[n, 0, t, 16:24, :], 0.0)]
 
         def blocks(v, first):
             return (
@@ -645,14 +676,19 @@
 
     lax.fori_loop(0, 2 * LT, fold, 0)
 
-    src = lax.broadcasted_iota(jnp.int32, (2 * LANES, 2 * LANES), 0)
-    dst = lax.broadcasted_iota(jnp.int32, (2 * LANES, 2 * LANES), 1)
+    coarse = lanes_of(8)
+    first = coarse // (2 * NCZ) * NZ + coarse % NCZ * BLK
+    first = jnp.concatenate(
+        [jnp.where(coarse // NCZ % 2 == half, first, -NZ) for half in range(2) for _ in range(NCZ)],
+        axis=0,
+    )
+    place = jnp.concatenate([rows_of(LANES)] * 2, axis=0)
     total = jnp.zeros((456, 2 * LANES), F32)
     for t in range(LT):
-        place = t * LANES + src % LANES
-        coarse = place // NZ * 2 * NCZ + src // LANES * NCZ + place % NZ // BLK
-        column = coarse + jnp.where(place % BLK == BLK - 1, LANES, 0)
-        pick = jnp.where(column == dst, 1.0, 0.0).astype(BF16)
+        step = place + t * LANES - first
+        inside = jnp.where((step >= 0) & (step < BLK - 1), 1.0, 0.0)
+        crossing = jnp.where(step == BLK - 1, 1.0, 0.0)
+        pick = jnp.concatenate([inside, crossing], axis=1).astype(BF16)
         for piece in halves(rows_in[t]):
             total = total + jnp.dot(piece, pick, preferred_element_type=F32)
     found[0:57, :] = jnp.sum(total.reshape(57, 8, 2 * LANES), axis=1)
@@ -740,8 +776,8 @@
     for n, (u, v) in enumerate(ACROSS):
         add(y_mat.at[v - u + 2], u, share(Y_ROW + n))
         add(z_mat.at[v - u + 2], u, share(Z_ROW + n))
-    for u in range(4):
-        add(rhs, u, share(RHS_ROW + u))
+    for u in range(-1, 5):
+        add(rhs, u, share(RHS_ROW + 1 + u))
     for block in range(2):
         inv[pl.ds(EDGE + block, count, 2), :] = OMEGA_COARSE * share(INVERSE_ROW + block)
     for step in range(1, 4):
@@ -776,16 +812,19 @@
 
 
 def finish_kernel(
-    count, near_rows, far_rows, got_a, got_b, smooth_in, w0_in, w1_in, w2_in, tx, ty, tz, k, b,
-    out, update, smooth, w0, w1, w2,
-    gathered, same, same_t, y_mat, y_mat_t, z_mat, z_mat_t, inv, rhs, e, e_y, e_z, strips, spread, first, second, tail_a, tail_b,
+    count, near_rows, far_rows, got_a, got_b,
+    smooth_in, w0_in, w1_in, w2_in, tx_in, ty_in, tz_in, k_in, b_in,
+    out, update, smooth, w0, w1, w2, tx, ty, tz, k, b,
+    result, own_update, out_sems, gathered, same, same_t, y_mat, y_mat_t, z_mat, z_mat_t, inv, rhs, e, e_y, e_z, strips, spread, first, second, tail_a, tail_b,
 ):
     weights = (w0, w1, w2)
     coarse_solve(
         count, (near_rows, far_rows), gathered, same, same_t, y_mat, y_mat_t, z_mat, z_mat_t, inv, rhs, e, e_y, e_z
     )
     base = EDGE + 2 * lax.axis_index("gx")
-    update[...] = e[pl.ds(base, 2), :]
+    own_update[...] = e[pl.ds(base, 2), :]
+    sent = pltpu.make_async_copy(own_update, update, out_sems.at[TILES // PHASES])
+    sent.start()
     near = {s: e[pl.ds(base + s, 1), :] for s in range(-2, 4)}
     row = rows_of(SPREAD)
     lane = lanes_of(SPREAD)
@@ -803,11 +842,9 @@
             turned = jnp.where(lane < 2 * NCZ, turned, lane_roll(rest, (2 - strip) * NCZ))
             turned = jnp.where(lane < 3 * NCZ, turned, 0.0)
             strips[a, strip] = turned.astype(BF16)
-    src = lax.broadcasted_iota(jnp.int32, (LANES, LANES), 0)
-    dst = lax.broadcasted_iota(jnp.int32, (LANES, LANES), 1)
     flat = strips[...].reshape(3 * NCY * SPREAD, LANES)
     for phase in range(PHASES):
-        pick = jnp.where((phase * LANES + dst) % NZ // BLK == src % NCZ, 1.0, 0.0).astype(BF16)
+        pick = z_blocks(phase, 1)
         got = jnp.dot(flat, pick, preferred_element_type=F32)
         spread[phase] = got.reshape(3, NCY, SPREAD, LANES)
 
@@ -822,6 +859,11 @@
             for a, w in enumerate(weights):
                 for n, row in enumerate(rows[1:]):
                     w[plane(w, row, q, size), :] = got[4 + 2 * a + n]
+            scale = jnp.where(got[11] > 0.0, OMEGA_FINE / got[11], 0.0)
+            for ref, value in ((k, scale), (b, scale * got[10]), (ty, got[12]), (tz, got[13])):
+                ref[plane(ref, rows[1], q, size), :] = value
+            if side == 0:
+                tx[plane(tx, rows[2], q, size), :] = got[14]
 
     def prolong(t, i, carry):
         n = t // PAIR
@@ -848,10 +890,21 @@
     def last(t, i, carry):
         total, after = coupled(first, tx, ty, tz, t, TOP, OWN, carry)
         here = span(t, TOP, OWN)
-        out[:, at(t)] = b[here, :] + (1.0 - OMEGA_FINE) * carry[0] + k[here, :] * total
+        result[:, at(t)] = b[here, :] + (1.0 - OMEGA_FINE) * carry[0] + k[here, :] * total
+        if i % PHASES == PHASES - 1:
+            part_out(t // PHASES).start()
         return after
 
-    over_tiles(last, coupled_start(first, TOP, OWN))
+    width = PHASES * LANES
+
+    def part_out(n):
+        lanes = pl.ds(pl.multiple_of(n * width, width), width)
+        return pltpu.make_async_copy(result.at[:, lanes], out.at[:, lanes], out_sems.at[n])
+
+    over_tiles(last, coupled_start(first, TOP, OWN), unroll=4)
+    for n in range(TILES // PHASES):
+        part_out(n).wait()
+    sent.wait()
 
 
 def finish(count, near_rows, far_rows, got_a, got_b, smooth, w0, w1, w2, tx, ty, tz, k, b):
@@ -866,11 +919,11 @@
             jax.ShapeDtypeStruct((OWN, PLANE), F32),
             jax.ShapeDtypeStruct((2, LANES), F32),
         )
-        + (padded(),) * 4,
+        + (padded(),) * 9,
         in_specs=in_vmem(13),
-        out_specs=tuple(in_vmem(6)),
-        input_output_aliases={n + 4: n + 2 for n in range(4)},
-        scratch_shapes=[vmem((count * ALL_ROWS, LANES))]
+        out_specs=tuple(in_hbm(2) + in_vmem(9)),
+        input_output_aliases={n + 4: n + 2 for n in range(9)},
+        scratch_shapes=[cells(F32), vmem((2, LANES)), semaphores(TILES // PHASES + 1), vmem((count * ALL_ROWS, LANES))]
         + [
             vmem((4, rows + 2 * EDGE, LANES)),
             vmem((3, rows, LANES)),
@@ -923,25 +976,30 @@
         low += ref.shape[0]
 
 
-def stacked(blocks):
+def stacked(blocks, after=()):
     rows = sum(block.shape[0] for block in blocks)
+
+    def kernel(*refs):
+        stacked_kernel(*refs[: len(blocks)], refs[-1])
+
     return pl.pallas_call(
-        stacked_kernel,
+        kernel,
         out_shape=vmem((rows, LANES)),
-        in_specs=in_vmem(len(blocks)),
+        in_specs=in_vmem(len(blocks)) + [pl.BlockSpec(memory_space=pl.ANY)] * len(after),
         out_specs=in_vmem(1)[0],
         compiler_params=params(4),
-    )(*blocks)
-
-
-def gather(rows):
+    )(*blocks, *after)
+
+
+def gather(rows, after):
     count = lax.axis_size("gx")
-    for steps in rounds(count):
+    order = rounds(count)
+    for n, steps in enumerate(order):
         blocks = [rows]
         for step in steps:
             blocks.append(lax.ppermute(rows, "gx", [(i, i ^ step) for i in range(count)]))
         if steps != (1,):
-            rows = stacked(blocks)
+            rows = stacked(blocks, after if n == len(order) - 2 else ())
     return blocks
 
 
@@ -954,12 +1012,11 @@
     )
     got_a, got_b = swapped(pay_a, pay_b)
     operator = assemble(*own_fields, coarse_inverse)
-    *own_fields, k, b, smooth, edges, pay_a, pay_b = presmooth(
+    *own_fields, k, b, smooth, part, pay_a, pay_b = presmooth(
         got_a, got_b, raw, *own_fields, operator
     )
     got_a, got_b = swapped(pay_a, pay_b)
-    part = restrict(smooth, raw, *own_fields, edges, operator)
-    near_rows, far_rows = gather(part)
+    near_rows, far_rows = gather(part, (got_a, got_b))
     tx, ty, tz, dg, w0, w1, w2 = own_fields
     return finish(
         count, near_rows, far_rows, got_a, got_b, smooth, w0, w1, w2, tx, ty, tz, k, b

time: 56.1 us -> 54.7 us (0.975)
  the two profiles are of different devices: /device:TPU:11 before, /device:TPU:0 now
where the time goes in v2:
time: 54.7 us; the launch traced here: 54.5 us
  Pallas kernels  26.1 us (48%)
  starting transfers between devices  13 us (24%)
  waiting for transfers between devices  12.2 us (22%)
  local copies, waits for them, and re-layouts  2.37 us (4%)
  between operations  0.88 us (2%)
    ppermute x5, waiting for transfers between devices, gather(): lax.ppermute(rows, 'gx', [(i, i ^ step) for i in range(count)])  12.1 us
    pallas_call x1, Pallas kernels, assemble(): pl.pallas_call(assemble_kernel, out_shape=vmem((ALL_ROWS, LANES)), in_spe...  8.25 us
    pallas_call x1, Pallas kernels, finish(): pl.pallas_call(kernel, out_shape=(jax.ShapeDtypeStruct((OWN, PLANE), F32)...  7.43 us
    ppermute x5, starting transfers between devices, gather(): lax.ppermute(rows, 'gx', [(i, i ^ step) for i in range(count)])  7.03 us
    pallas_call x1, Pallas kernels, presmooth(): pl.pallas_call(presmooth_kernel, out_shape=(padded(),) * 10 + (vmem((ALL_...  6.16 us
    ppermute x2, starting transfers between devices, swapped(): got_a = lax.ppermute(pay_a, 'gx', [(i, i ^ 1) for i in range(count)])  4.46 us
    pallas_call x1, Pallas kernels, prepare(): pl.pallas_call(prepare_kernel, out_shape=(padded(),) * 8 + (payload(FIRST...  4.18 us
    unnamed x3, local copies, waits for them, and re-layouts  2.37 us
  transfers between devices with their start and end apart: 9, of which 3 were waited for; matrix products, arithmetic and copies ran while one was open for 0% of the time, Pallas kernels for 15%

profile of v2, /device:TPU:0, one launch (start us, length us, event | category | flops | bytes accessed | tf_op | source)
XLA Modules:
  0.0 54.5 jit_solution(17974250824034767097)
XLA Ops:
  0.6 2.4 %copy.26.side_in = bf16[2,20,12800]{2,1,0:T(8,128)(2,1)} copy(bf16[2,20,12800]{2,0,1:T(2,128)(2,1)} %param.14) | data formatting | bytes 2048000 | tf_op args[6]
  3.0 0.0 copy-start
  3.0 4.2 %shard_map.95 = (f32[2608,128]{1,0:T(8,128)S(1)}, f32[2608,128]{1,0:T(8,128)S(1)}, f32[2608,128]{1,0:T(8,128)S(1)}, f32[2608,128]{1,0:T(8,128)S(1)}, f32[2608,12...) custom-call(f32[20,12800]{1,0:T(8,128)} %rhs_in.1, ...), custom_call_target="tpu_custom_call" | custom-call | bytes 21000000 | tf_op jit(solution)/shard_map/pallas_call | solution.py:334
  7.2 0.5 collective-permute-start
  7.7 0.7 %collective-permute-start.1 = (bf16[1200,128]{1,0:T(8,128)(2,1)}, bf16[1200,128]{1,0:T(8,128)(2,1)S(1)}, u32[]{:S(2)}, u32[]{:S(2)}) collective-permute-start(bf16[1200,128]{1,0:T(8,128)(2,1)} %get-tuple-element.27), channel_id=1, source_target_pairs={{1,2},{2,1},{3,4},{4,3},{5,6},{6,5},{7,8},{8,7},{9,10},{10,9},{11,... | collective-permute-start | bytes 921608 | tf_op jit(solution)/shard_map/ppermute | solution.py:952
  8.4 0.0 copy-done
  8.4 8.2 %shard_map.96.operator = f32[56,128]{1,0:T(8,128)S(1)} custom-call(f32[2608,128]{1,0:T(8,128)S(1)} %get-tuple-element.29.tx_n.tx_in, f32[2608,128]{1,0:T(8,128)S(1)} %get-tuple-element.30.ty_n.ty_in, f32[2608,128]{1,0:T(8,128)S(1)} %get-tuple-element.31.tz_n.tz_in, f32[2608,128]{1,0:T(8,128)S(1)} %get-tuple-element.32.dg_n.dg_in, ...), custom_call_target="tpu_custom_call" | custom-call | bytes 35000000 | tf_op jit(solution)/shard_map/pallas_call | solution.py:733
  16.6 0.0 collective-permute-done.got_a
  16.7 0.0 collective-permute-done.1.got_b
  16.7 6.2 %shard_map.97 = (f32[2608,128]{1,0:T(8,128)S(1)}, f32[2608,128]{1,0:T(8,128)S(1)}, f32[2608,128]{1,0:T(8,128)S(1)}, f32[2608,128]{1,0:T(8,128)S(1)}, f32[2608,12...) custom-call(bf16[1200,128]{1,0:T(8,128)(2,1)S(1)} %collective-permut, ...), custom_call_target="tpu_custom_call", output_to_operand_aliasing={{0}: (3, {}), {1}: (4, {}), {2}: (5, {}), {3}: (6, {}), {4}... | custom-call | bytes 28000000 | tf_op jit(solution)/shard_map/pallas_call | solution.py:502
  22.8 3.9 %collective-permute-start.6 = (bf16[1504,128]{1,0:T(8,128)(2,1)S(1)}, bf16[1504,128]{1,0:T(8,128)(2,1)S(1)}, u32[]{:S(2)}, u32[]{:S(2)}) collective-permute-start(bf16[1504,128]{1,0:T(8,128)(2,1)S(1)} %get-tuple-element.37), channel_id=1, source_target_pairs={{0,1},{1,0},{2,3},{3,2},{4,5},{5,4},{6,7},{7,6},{8,9},{9,8},{10,11... | collective-permute-start | bytes 1155080 | tf_op jit(solution)/shard_map/ppermute | solution.py:950
  26.8 0.9 %collective-permute-start.7 = (bf16[1504,128]{1,0:T(8,128)(2,1)S(1)}, bf16[1504,128]{1,0:T(8,128)(2,1)S(1)}, u32[]{:S(2)}, u32[]{:S(2)}) collective-permute-start(bf16[1504,128]{1,0:T(8,128)(2,1)S(1)} %get-tuple-element.38), channel_id=1, source_target_pairs={{1,2},{2,1},{3,4},{4,3},{5,6},{6,5},{7,8},{8,7},{9,10},{10,9},{11,... | collective-permute-start | bytes 1155080 | tf_op jit(solution)/shard_map/ppermute | solution.py:952
  27.6 6.2 %collective-permute-start.4 = (f32[56,128]{1,0:T(8,128)S(1)}, f32[56,128]{1,0:T(8,128)S(1)}, u32[]{:S(2)}, u32[]{:S(2)}) collective-permute-start(f32[56,128]{1,0:T(8,128)S(1)} %get-tuple-element.36.refs_0_), channel_id=1, source_target_pairs={{0,12},{1,13},{2,14},{3,15},{4,8},{5,9},{6,10},{7,11},{8,4},{9,5},... | collective-permute-start | bytes 86024 | tf_op jit(solution)/shard_map/ppermute | solution.py:1000
  33.9 0.0 collective-permute-start.3
  33.9 0.6 %collective-permute-start.2 = (f32[56,128]{1,0:T(8,128)S(1)}, f32[56,128]{1,0:T(8,128)S(1)}, u32[]{:S(2)}, u32[]{:S(2)}) collective-permute-start(f32[56,128]{1,0:T(8,128)S(1)} %get-tuple-element.36.refs_0_), channel_id=1, source_target_pairs={{0,4},{1,5},{2,6},{3,7},{4,0},{5,1},{6,2},{7,3},{8,12},{9,13},{10,... | collective-permute-start | bytes 86024 | tf_op jit(solution)/shard_map/ppermute | solution.py:1000
  34.5 5.9 %collective-permute-done.4.refs_3_ = f32[56,128]{1,0:T(8,128)S(1)} collective-permute-done((f32[56,128]{1,0:T(8,128)S(1)}, f32[56,128]{1,0:T(8,128)S(1)}, u32[]{:S(2)}, u32[]{:S(2)}) %collective-permute-start.4) | collective-permute-done | bytes 28704 | tf_op jit(solution)/shard_map/ppermute | solution.py:1000
  40.4 0.0 collective-permute-done.3.refs_2_
  40.4 0.0 collective-permute-done.2.refs_1_
  40.4 0.1 collective-permute-start.5
  40.5 4.8 %collective-permute-done.5.refs_1_ = f32[224,128]{1,0:T(8,128)S(1)} collective-permute-done((f32[224,128]{1,0:T(8,128)S(1)}, f32[224,128]{1,0:T(8,128)S(1)}, u32[]{:S(2)}, u32[]{:S(2)}) %collective-permute-start.5) | collective-permute-done | bytes 114720 | tf_op jit(solution)/shard_map/ppermute | solution.py:1000
  45.3 0.0 collective-permute-done.6.refs_2_
  45.3 0.0 collective-permute-done.7.refs_3_
  45.3 0.1 collective-permute-start.8
  45.4 1.5 %collective-permute-done.8.refs_1_ = f32[448,128]{1,0:T(8,128)S(1)} collective-permute-done((f32[448,128]{1,0:T(8,128)S(1)}, f32[448,128]{1,0:T(8,128)S(1)}, u32[]{:S(2)}, u32[]{:S(2)}) %collective-permute-start.8) | collective-permute-done | bytes 229408 | tf_op jit(solution)/shard_map/ppermute | solution.py:1000
  46.9 7.4 %shard_map.100 = (f32[20,12800]{1,0:T(8,128)}, f32[2,128]{1,0:T(2,128)}, f32[2608,128]{1,0:T(8,128)S(1)}, f32[2608,128]{1,0:T(8,128)S(1)}, f32[2608,128]{1,0:T(8...) custom-call(f32[448,128]{1,0:T(8,128)S(1)} %shard_map.99.refs_0_, ...), custom_call_target="tpu_custom_call", output_to_operand_aliasing={{2}: (4, {}), {3}: (5, {}), {4}: (6, {}), {5}: (7, {}), {6}... | custom-call | bytes 42000000 | tf_op jit(solution)/shard_map/pallas_call | solution.py:916
  (2 shorter events, 0.0 us)
Async XLA Ops:
  3.0 5.4 %copy-start = (f32[2,128]{1,0:T(2,128)S(1)}, f32[2,128]{1,0:T(2,128)}, u32[]{:S(2)}) copy-start(f32[2,128]{1,0:T(2,128)} %inverse.1) | copy-start | bytes 3076
  7.2 9.5 %collective-permute-start = (bf16[1200,128]{1,0:T(8,128)(2,1)}, bf16[1200,128]{1,0:T(8,128)(2,1)S(1)}, u32[]{:S(2)}, u32[]{:S(2)}) collective-permute-start(bf16[1200,128]{1,0:T(8,128)(2,1)} %get-tuple-element.26), channel_id=1, source_target_pairs={{0,1},{1,0},{2,3},{3,2},{4,5},{5,4},{6,7},{7,6},{8,9},{9,8},{10,11... | collective-permute-start | bytes 921608 | tf_op jit(solution)/shard_map/ppermute | solution.py:950
  7.7 9.0 %collective-permute-start.1 = (bf16[1200,128]{1,0:T(8,128)(2,1)}, bf16[1200,128]{1,0:T(8,128)(2,1)S(1)}, u32[]{:S(2)}, u32[]{:S(2)}) collective-permute-start(bf16[1200,128]{1,0:T(8,128)(2,1)} %get-tuple-element.27), channel_id=1, source_target_pairs={{1,2},{2,1},{3,4},{4,3},{5,6},{6,5},{7,8},{8,7},{9,10},{10,9},{11,... | collective-permute-start | bytes 921608 | tf_op jit(solution)/shard_map/ppermute | solution.py:952
  22.8 22.5 %collective-permute-start.6 = (bf16[1504,128]{1,0:T(8,128)(2,1)S(1)}, bf16[1504,128]{1,0:T(8,128)(2,1)S(1)}, u32[]{:S(2)}, u32[]{:S(2)}) collective-permute-start(bf16[1504,128]{1,0:T(8,128)(2,1)S(1)} %get-tuple-element.37), channel_id=1, source_target_pairs={{0,1},{1,0},{2,3},{3,2},{4,5},{5,4},{6,7},{7,6},{8,9},{9,8},{10,11... | collective-permute-start | bytes 1155080 | tf_op jit(solution)/shard_map/ppermute | solution.py:950
  26.8 18.5 %collective-permute-start.7 = (bf16[1504,128]{1,0:T(8,128)(2,1)S(1)}, bf16[1504,128]{1,0:T(8,128)(2,1)S(1)}, u32[]{:S(2)}, u32[]{:S(2)}) collective-permute-start(bf16[1504,128]{1,0:T(8,128)(2,1)S(1)} %get-tuple-element.38), channel_id=1, source_target_pairs={{1,2},{2,1},{3,4},{4,3},{5,6},{6,5},{7,8},{8,7},{9,10},{10,9},{11,... | collective-permute-start | bytes 1155080 | tf_op jit(solution)/shard_map/ppermute | solution.py:952
  27.6 12.8 %collective-permute-start.4 = (f32[56,128]{1,0:T(8,128)S(1)}, f32[56,128]{1,0:T(8,128)S(1)}, u32[]{:S(2)}, u32[]{:S(2)}) collective-permute-start(f32[56,128]{1,0:T(8,128)S(1)} %get-tuple-element.36.refs_0_), channel_id=1, source_target_pairs={{0,12},{1,13},{2,14},{3,15},{4,8},{5,9},{6,10},{7,11},{8,4},{9,5},... | collective-permute-start | bytes 86024 | tf_op jit(solution)/shard_map/ppermute | solution.py:1000
  33.9 6.5 %collective-permute-start.3 = (f32[56,128]{1,0:T(8,128)S(1)}, f32[56,128]{1,0:T(8,128)S(1)}, u32[]{:S(2)}, u32[]{:S(2)}) collective-permute-start(f32[56,128]{1,0:T(8,128)S(1)} %get-tuple-element.36.refs_0_), channel_id=1, source_target_pairs={{0,8},{1,9},{2,10},{3,11},{4,12},{5,13},{6,14},{7,15},{8,0},{9,1},... | collective-permute-start | bytes 86024 | tf_op jit(solution)/shard_map/ppermute | solution.py:1000
  33.9 6.5 %collective-permute-start.2 = (f32[56,128]{1,0:T(8,128)S(1)}, f32[56,128]{1,0:T(8,128)S(1)}, u32[]{:S(2)}, u32[]{:S(2)}) collective-permute-start(f32[56,128]{1,0:T(8,128)S(1)} %get-tuple-element.36.refs_0_), channel_id=1, source_target_pairs={{0,4},{1,5},{2,6},{3,7},{4,0},{5,1},{6,2},{7,3},{8,12},{9,13},{10,... | collective-permute-start | bytes 86024 | tf_op jit(solution)/shard_map/ppermute | solution.py:1000
  40.4 4.9 %collective-permute-start.5 = (f32[224,128]{1,0:T(8,128)S(1)}, f32[224,128]{1,0:T(8,128)S(1)}, u32[]{:S(2)}, u32[]{:S(2)}) collective-permute-start(f32[224,128]{1,0:T(8,128)S(1)} %shard_map.98.refs_0_), channel_id=1, source_target_pairs={{0,2},{1,3},{2,0},{3,1},{4,6},{5,7},{6,4},{7,5},{8,10},{9,11},{10,... | collective-permute-start | bytes 344072 | tf_op jit(solution)/shard_map/ppermute | solution.py:1000
  45.3 1.6 %collective-permute-start.8 = (f32[448,128]{1,0:T(8,128)S(1)}, f32[448,128]{1,0:T(8,128)S(1)}, u32[]{:S(2)}, u32[]{:S(2)}) collective-permute-start(f32[448,128]{1,0:T(8,128)S(1)} %shard_map.99.refs_0_), channel_id=1, source_target_pairs={{0,1},{1,0},{2,3},{3,2},{4,5},{5,4},{6,7},{7,6},{8,9},{9,8},{10,11... | collective-permute-start | bytes 688136 | tf_op jit(solution)/shard_map/ppermute | solution.py:1000

commit v3 on v2

--- a/solution.py
+++ b/solution.py
@@ -42,8 +42,9 @@
 Y_ROW = len(SAME)
 Z_ROW = Y_ROW + len(ACROSS)
 INVERSE_ROW = Z_ROW + len(ACROSS)
-RHS_ROW = INVERSE_ROW + 2
-ALL_ROWS = 56
+RHS_ROW = INVERSE_ROW + 1
+ALL_ROWS = 48
+TAIL = COARSE - NCZ
 EDGES = 24
 F32 = jnp.float32
 BF16 = jnp.bfloat16
@@ -93,7 +94,7 @@
     def copy(field, n):
         lanes = pl.ds(pl.multiple_of(n * width, width), width)
         return pltpu.make_async_copy(
-            sources[field].at[:, lanes], buffers[field].at[:, lanes], sems.at[field, n]
+            sources[field].at[..., lanes], buffers[field].at[..., lanes], sems.at[field, n]
         )
 
     for n in range(PAIRS):
@@ -278,11 +279,11 @@
 def prepare_kernel(
     rhs_in, accum_in, x_in, y_in, z_in, center_in, side_in,
     raw, tx_n, ty_n, tz_n, dg_n, w0_n, w1_n, w2_n, pay_a, pay_b,
-    rhs_v, accum_v, x_v, y_v, z_v, center_v, lower_v, upper_v, tail_a, tail_b, sems,
+    rhs_v, accum_v, x_v, y_v, z_v, center_v, side_v, mixed, tail_a, tail_b, sems,
 ):
     wait = stream(
-        (rhs_in, accum_in, x_in, y_in, z_in, center_in, side_in.at[0], side_in.at[1]),
-        (rhs_v, accum_v, x_v, y_v, z_v, center_v, lower_v, upper_v),
+        (rhs_in, accum_in, x_in, y_in, z_in, center_in, side_in),
+        (rhs_v, accum_v, x_v, y_v, z_v, center_v, side_v),
         sems,
     )
     weights = (w0_n, w1_n, w2_n)
@@ -290,8 +291,12 @@
 
     def load(t, i, carry):
         z_before, y_before, y_second = carry
-        for ref, src in zip(weights, (center_v, lower_v, upper_v)):
-            ref[span(t, TOP, OWN), :] = own(src, t)
+        w0_n[span(t, TOP, OWN), :] = own(center_v, t)
+        for x in range(OWN):
+            low = i * 2 * OWN + 2 * x
+            mixed[low : low + 2, :] = side_v[x, :, at(t)].astype(F32)
+        for n, ref in enumerate((w1_n, w2_n)):
+            ref[span(t, TOP, OWN), :] = mixed[pl.ds(i * 2 * OWN + n, OWN, 2), :]
         z_pos = (i * LANES + lane) % NZ
         cells = t * LANES + lane
         here = span(t, TOP, OWN)
@@ -312,7 +317,7 @@
         return z_rolled, y_rolled, y_before
 
     zero = lanes_of(OWN).astype(F32) * 0.0
-    over_tiles(load, (zero, zero, zero), wait)
+    over_tiles(load, (zero, zero, zero), wait, unroll=4)
 
     def first_sweep(row):
         r, d = read_plane(raw, row), read_plane(dg_n, row)
@@ -336,7 +341,11 @@
         out_shape=(padded(),) * 8 + (payload(FIRST),) * 2,
         in_specs=in_hbm(7),
         out_specs=tuple(in_vmem(10)),
-        scratch_shapes=[cells(F32)] + [cells()] * 7 + tails(FIRST) + [semaphores(8, PAIRS)],
+        scratch_shapes=[cells(F32)]
+        + [cells()] * 5
+        + [vmem((OWN, 2, PLANE), BF16), vmem((PAIR * 2 * OWN, LANES))]
+        + tails(FIRST)
+        + [semaphores(7, PAIRS)],
         compiler_params=params(46),
         cost_estimate=lasting(6),
     )(*fields)
@@ -352,10 +361,10 @@
 
 
 def presmooth_kernel(
-    got_a, got_b, raw, tx_in, ty_in, tz_in, dg_in, w0_in, w1_in, w2_in, operator,
+    got_a, got_b, raw, tx_in, ty_in, tz_in, dg_in, w0_in, w1_in, w2_in, after,
     tx, ty, tz, dg, w0, w1, w2,
-    k, b, smooth, part, pay_a, pay_b,
-    work, tail_a, tail_b, second_a, second_b, edges, sums, rest, shares_v,
+    k, b, smooth, edges, pay_a, pay_b,
+    work, tail_a, tail_b, second_a, second_b,
 ):
     weights = (w0, w1, w2)
     both = received(FIRST, got_a, got_b, tail_a, tail_b)
@@ -426,6 +435,24 @@
 
     send_both(pay_a, pay_b, second_a, second_b, planes(LAST), planes(HEAD))
 
+
+def presmooth(got_a, got_b, raw, tx, ty, tz, dg, w0, w1, w2, operator):
+    return pl.pallas_call(
+        presmooth_kernel,
+        out_shape=(padded(),) * 10 + (vmem((TILES * EDGES, LANES)),) + (payload(SECOND),) * 2,
+        in_specs=in_vmem(11),
+        out_specs=tuple(in_vmem(13)),
+        input_output_aliases={n + 3: n for n in range(7)},
+        scratch_shapes=[padded()] + tails(FIRST) + tails(SECOND),
+        compiler_params=params(8),
+        cost_estimate=lasting(4),
+    )(got_a, got_b, raw, tx, ty, tz, dg, w0, w1, w2, operator)
+
+
+def restrict_kernel(
+    smooth, raw, tx, ty, tz, dg, w0, w1, w2, edges, operator, part, sums, rest, shares_v
+):
+    weights = (w0, w1, w2)
     rows = 48 + EDGES
     lane = lanes_of(rows)
     row8 = rows_of(8)
@@ -498,25 +525,20 @@
             part[row : row + 1, :] += placed[low + a : low + a + 1]
 
 
-def presmooth(got_a, got_b, raw, tx, ty, tz, dg, w0, w1, w2, operator):
+def restrict(smooth, raw, tx, ty, tz, dg, w0, w1, w2, edges, operator):
     return pl.pallas_call(
-        presmooth_kernel,
-        out_shape=(padded(),) * 10 + (vmem((ALL_ROWS, LANES)),) + (payload(SECOND),) * 2,
+        restrict_kernel,
+        out_shape=vmem((ALL_ROWS, LANES)),
         in_specs=in_vmem(11),
-        out_specs=tuple(in_vmem(13)),
-        input_output_aliases={n + 3: n for n in range(7)},
-        scratch_shapes=[padded()]
-        + tails(FIRST)
-        + tails(SECOND)
-        + [
-            vmem((TILES * EDGES, LANES)),
+        out_specs=in_vmem(1)[0],
+        scratch_shapes=[
             vmem((PHASES, NCY, 48 + EDGES, LANES)),
             vmem((PAIR * 24, LANES)),
             vmem((TILES * (48 + EDGES), LANES)),
         ],
-        compiler_params=params(14),
-        cost_estimate=lasting(8),
-    )(got_a, got_b, raw, tx, ty, tz, dg, w0, w1, w2, operator)
+        compiler_params=params(10),
+        cost_estimate=lasting(3),
+    )(smooth, raw, tx, ty, tz, dg, w0, w1, w2, edges, operator)
 
 
 def regrouped(ref, dst, shift, index, load, cut=False):
@@ -725,7 +747,12 @@
         for n, pair in enumerate(pairs):
             if pair in kept:
                 out[first + n : first + n + 1, :] = kept[pair]
-    out[INVERSE_ROW : INVERSE_ROW + 2, :] = inverse[...]
+    out[INVERSE_ROW : INVERSE_ROW + 1, :] = inverse[0:1, :]
+    lane = lanes_of(1)
+    for n in range(NCY):
+        row = Y_ROW + n
+        moved = lane_roll(inverse[1:2, :], TAIL - n * NCZ)
+        out[row : row + 1, :] = jnp.where(lane < TAIL, out[row : row + 1, :], moved)
 
 
 def assemble(tx, ty, tz, dg, w0, w1, w2, inverse):
@@ -773,13 +800,19 @@
 
     for n, (u, v) in enumerate(SAME):
         add(same.at[v - u], u, share(n))
+    lane = lanes_of(count)
+    second = jnp.zeros((count, LANES), F32)
     for n, (u, v) in enumerate(ACROSS):
-        add(y_mat.at[v - u + 2], u, share(Y_ROW + n))
+        value = share(Y_ROW + n)
+        add(y_mat.at[v - u + 2], u, jnp.where(lane < TAIL, value, 0.0))
+        if n < NCY:
+            moved = lane_roll(value, n * NCZ - TAIL)
+            second = jnp.where((lane >= n * NCZ) & (lane < n * NCZ + NCZ), moved, second)
         add(z_mat.at[v - u + 2], u, share(Z_ROW + n))
     for u in range(-1, 5):
         add(rhs, u, share(RHS_ROW + 1 + u))
-    for block in range(2):
-        inv[pl.ds(EDGE + block, count, 2), :] = OMEGA_COARSE * share(INVERSE_ROW + block)
+    inv[pl.ds(EDGE, count, 2), :] = OMEGA_COARSE * share(INVERSE_ROW)
+    inv[pl.ds(EDGE + 1, count, 2), :] = OMEGA_COARSE * second
     for step in range(1, 4):
         same_t[step - 1] = same[step, pl.ds(EDGE - step, rows), :]
     for step in range(-2, 3):
@@ -1008,14 +1041,16 @@
 ):
     count = lax.axis_size("gx")
     raw, *own_fields, pay_a, pay_b = prepare(
-        rhs, accumulation, trans_x, trans_y, trans_z, basis_center, basis_side
+        rhs, accumulation, trans_x, trans_y, trans_z, basis_center,
+        basis_side.transpose(1, 0, 2),
     )
     got_a, got_b = swapped(pay_a, pay_b)
     operator = assemble(*own_fields, coarse_inverse)
-    *own_fields, k, b, smooth, part, pay_a, pay_b = presmooth(
+    *own_fields, k, b, smooth, edges, pay_a, pay_b = presmooth(
         got_a, got_b, raw, *own_fields, operator
     )
     got_a, got_b = swapped(pay_a, pay_b)
+    part = restrict(smooth, raw, *own_fields, edges, operator)
     near_rows, far_rows = gather(part, (got_a, got_b))
     tx, ty, tz, dg, w0, w1, w2 = own_fields
     return finish(

time: 54.7 us -> 50.7 us (0.927)
  waiting for transfers between devices: 12.2 us -> 9.51 us
  local copies, waits for them, and re-layouts: 2.37 us -> 0.01 us
  starting transfers between devices: 13 us -> 13.6 us
    ppermute x5, waiting for transfers between devices: 12.1 us -> 9.5 us  [gather(): lax.ppermute(rows, 'gx', [(i, i ^ step) for i in range(count)])]
    unnamed x3 -> x2, local copies, waits for them, and re-layouts: 2.37 us -> 0.01 us
    ppermute x5, starting transfers between devices: 7.03 us -> 7.66 us  [gather(): lax.ppermute(rows, 'gx', [(i, i ^ step) for i in range(count)])]
    pallas_call x1 -> x2, Pallas kernels: 6.16 us -> 6.17 us  [the longest x1 3.49 us: presmooth(): pl.pallas_call(presmooth_kernel, out_shape=(padded(),) * 10 + (vmem((TILE...]
  transfers between devices with their start and end apart: 9 -> 9, of which waited for: 3 -> 4; matrix products, arithmetic and copies ran while one was open for 0% -> 0% of each run, Pallas kernels for 15% -> 22%
where the time goes in v3:
time: 50.7 us; the launch traced here: 50.6 us
  Pallas kernels  26.5 us (52%)
  starting transfers between devices  13.6 us (27%)
  waiting for transfers between devices  9.51 us (19%)
  between operations  0.89 us (2%)
    ppermute x5, waiting for transfers between devices, gather(): lax.ppermute(rows, 'gx', [(i, i ^ step) for i in range(count)])  9.5 us
    pallas_call x1, Pallas kernels, assemble(): pl.pallas_call(assemble_kernel, out_shape=vmem((ALL_ROWS, LANES)), in_spe...  8.24 us
    ppermute x5, starting transfers between devices, gather(): lax.ppermute(rows, 'gx', [(i, i ^ step) for i in range(count)])  7.66 us
    pallas_call x1, Pallas kernels, finish(): pl.pallas_call(kernel, out_shape=(jax.ShapeDtypeStruct((OWN, PLANE), F32)...  7.56 us
    pallas_call x1, Pallas kernels, prepare(): pl.pallas_call(prepare_kernel, out_shape=(padded(),) * 8 + (payload(FIRST...  4.55 us
    ppermute x2, starting transfers between devices, swapped(): got_a = lax.ppermute(pay_a, 'gx', [(i, i ^ 1) for i in range(count)])  4.46 us
    pallas_call x1, Pallas kernels, presmooth(): pl.pallas_call(presmooth_kernel, out_shape=(padded(),) * 10 + (vmem((TILE...  3.49 us
    pallas_call x1, Pallas kernels, restrict(): pl.pallas_call(restrict_kernel, out_shape=vmem((ALL_ROWS, LANES)), in_spe...  2.68 us
  transfers between devices with their start and end apart: 9, of which 4 were waited for; matrix products, arithmetic and copies ran while one was open for 0% of the time, Pallas kernels for 22%

profile of v3, /device:TPU:0, one launch (start us, length us, event | category | flops | bytes accessed | tf_op | source)
XLA Modules:
  0.0 50.6 jit_solution(8569799018866704891)
XLA Ops:
  0.6 0.0 copy-start
  0.6 4.5 %shard_map.95 = (f32[2608,128]{1,0:T(8,128)S(1)}, f32[2608,128]{1,0:T(8,128)S(1)}, f32[2608,128]{1,0:T(8,128)S(1)}, f32[2608,128]{1,0:T(8,128)S(1)}, f32[2608,12...) custom-call(f32[20,12800]{1,0:T(8,128)} %rhs_in.1, ...), custom_call_target="tpu_custom_call" | custom-call | bytes 21000000 | tf_op jit(solution)/shard_map/pallas_call | solution.py:339
  5.2 0.5 %collective-permute-start = (bf16[1200,128]{1,0:T(8,128)(2,1)}, bf16[1200,128]{1,0:T(8,128)(2,1)S(1)}, u32[]{:S(2)}, u32[]{:S(2)}) collective-permute-start(bf16[1200,128]{1,0:T(8,128)(2,1)} %get-tuple-element.27), channel_id=1, source_target_pairs={{0,1},{1,0},{2,3},{3,2},{4,5},{5,4},{6,7},{7,6},{8,9},{9,8},{10,11... | collective-permute-start | bytes 921608 | tf_op jit(solution)/shard_map/ppermute | solution.py:983
  5.7 0.7 %collective-permute-start.1 = (bf16[1200,128]{1,0:T(8,128)(2,1)}, bf16[1200,128]{1,0:T(8,128)(2,1)S(1)}, u32[]{:S(2)}, u32[]{:S(2)}) collective-permute-start(bf16[1200,128]{1,0:T(8,128)(2,1)} %get-tuple-element.28), channel_id=1, source_target_pairs={{1,2},{2,1},{3,4},{4,3},{5,6},{6,5},{7,8},{8,7},{9,10},{10,9},{11,... | collective-permute-start | bytes 921608 | tf_op jit(solution)/shard_map/ppermute | solution.py:985
  6.4 0.0 copy-done
  6.4 8.2 %shard_map.96.after.operator = f32[48,128]{1,0:T(8,128)S(1)} custom-call(f32[2608,128]{1,0:T(8,128)S(1)} %get-tuple-element.30.tx_n.tx_in, f32[2608,128]{1,0:T(8,128)S(1)} %get-tuple-element.31.ty_n.ty_in, f32[2608,128]{1,0:T(8,128)S(1)} %get-tuple-element.32.tz_n.tz_in, f32[2608,128]{1,0:T(8,128)S(1)} %get-tuple-element.33.dg_n.dg_in, ...), custom_call_target="tpu_custom_call" | custom-call | bytes 35000000 | tf_op jit(solution)/shard_map/pallas_call | solution.py:760
  14.6 0.0 collective-permute-done.got_a
  14.7 0.0 collective-permute-done.1.got_b
  14.7 3.5 %shard_map.97 = (f32[2608,128]{1,0:T(8,128)S(1)}, f32[2608,128]{1,0:T(8,128)S(1)}, f32[2608,128]{1,0:T(8,128)S(1)}, f32[2608,128]{1,0:T(8,128)S(1)}, f32[2608,12...) custom-call(bf16[1200,128]{1,0:T(8,128)(2,1)S(1)} %collective-permut, ...), custom_call_target="tpu_custom_call", output_to_operand_aliasing={{0}: (3, {}), {1}: (4, {}), {2}: (5, {}), {3}: (6, {}), {4}... | custom-call | bytes 14000000 | tf_op jit(solution)/shard_map/pallas_call | solution.py:440
  18.2 3.9 %collective-permute-start.6 = (bf16[1504,128]{1,0:T(8,128)(2,1)S(1)}, bf16[1504,128]{1,0:T(8,128)(2,1)S(1)}, u32[]{:S(2)}, u32[]{:S(2)}) collective-permute-start(bf16[1504,128]{1,0:T(8,128)(2,1)S(1)} %get-tuple-element.46), channel_id=1, source_target_pairs={{0,1},{1,0},{2,3},{3,2},{4,5},{5,4},{6,7},{7,6},{8,9},{9,8},{10,11... | collective-permute-start | bytes 1155080 | tf_op jit(solution)/shard_map/ppermute | solution.py:983
  22.1 0.9 %collective-permute-start.7 = (bf16[1504,128]{1,0:T(8,128)(2,1)S(1)}, bf16[1504,128]{1,0:T(8,128)(2,1)S(1)}, u32[]{:S(2)}, u32[]{:S(2)}) collective-permute-start(bf16[1504,128]{1,0:T(8,128)(2,1)S(1)} %get-tuple-element.47), channel_id=1, source_target_pairs={{1,2},{2,1},{3,4},{4,3},{5,6},{6,5},{7,8},{8,7},{9,10},{10,9},{11,... | collective-permute-start | bytes 1155080 | tf_op jit(solution)/shard_map/ppermute | solution.py:985
  23.0 2.7 %shard_map.98.refs_0_ = f32[48,128]{1,0:T(8,128)S(1)} custom-call(f32[2608,128]{1,0:T(8,128)S(1)} %get-tuple-element.37.smooth.refs_4_, f32[2608,128]{1,0:T(8,128)S(1)} %get-tuple-element.29.raw, f32[2608,128]{1,0:T(8,128)S(1)} %get-tuple-element.38.tx.refs_8_, f32[2608,128]{1,0:T(8,128)S(1)} %get-tuple-element.39.ty.refs_9_, ...), custom_call_target="tpu_custom_call" | custom-call | bytes 10500000 | tf_op jit(solution)/shard_map/pallas_call | solution.py:529
  25.7 6.3 %collective-permute-start.4 = (f32[48,128]{1,0:T(8,128)S(1)}, f32[48,128]{1,0:T(8,128)S(1)}, u32[]{:S(2)}, u32[]{:S(2)}) collective-permute-start(f32[48,128]{1,0:T(8,128)S(1)} %shard_map.98.refs_0_), channel_id=1, source_target_pairs={{0,12},{1,13},{2,14},{3,15},{4,8},{5,9},{6,10},{7,11},{8,4},{9,5},... | collective-permute-start | bytes 73736 | tf_op jit(solution)/shard_map/ppermute | solution.py:1033
  31.9 0.0 collective-permute-start.3
  31.9 0.6 %collective-permute-start.2 = (f32[48,128]{1,0:T(8,128)S(1)}, f32[48,128]{1,0:T(8,128)S(1)}, u32[]{:S(2)}, u32[]{:S(2)}) collective-permute-start(f32[48,128]{1,0:T(8,128)S(1)} %shard_map.98.refs_0_), channel_id=1, source_target_pairs={{0,4},{1,5},{2,6},{3,7},{4,0},{5,1},{6,2},{7,3},{8,12},{9,13},{10,... | collective-permute-start | bytes 73736 | tf_op jit(solution)/shard_map/ppermute | solution.py:1033
  32.5 2.9 %collective-permute-done.4.refs_3_ = f32[48,128]{1,0:T(8,128)S(1)} collective-permute-done((f32[48,128]{1,0:T(8,128)S(1)}, f32[48,128]{1,0:T(8,128)S(1)}, u32[]{:S(2)}, u32[]{:S(2)}) %collective-permute-start.4) | collective-permute-done | bytes 24608 | tf_op jit(solution)/shard_map/ppermute | solution.py:1033
  35.4 1.2 %collective-permute-done.3.refs_2_ = f32[48,128]{1,0:T(8,128)S(1)} collective-permute-done((f32[48,128]{1,0:T(8,128)S(1)}, f32[48,128]{1,0:T(8,128)S(1)}, u32[]{:S(2)}, u32[]{:S(2)}) %collective-permute-start.3) | collective-permute-done | bytes 24608 | tf_op jit(solution)/shard_map/ppermute | solution.py:1033
  36.6 0.0 collective-permute-done.2.refs_1_
  36.6 0.7 %collective-permute-start.5 = (f32[192,128]{1,0:T(8,128)S(1)}, f32[192,128]{1,0:T(8,128)S(1)}, u32[]{:S(2)}, u32[]{:S(2)}) collective-permute-start(f32[192,128]{1,0:T(8,128)S(1)} %shard_map.99.refs_0_), channel_id=1, source_target_pairs={{0,2},{1,3},{2,0},{3,1},{4,6},{5,7},{6,4},{7,5},{8,10},{9,11},{10,... | collective-permute-start | bytes 294920 | tf_op jit(solution)/shard_map/ppermute | solution.py:1033
  37.3 4.0 %collective-permute-done.5.refs_1_ = f32[192,128]{1,0:T(8,128)S(1)} collective-permute-done((f32[192,128]{1,0:T(8,128)S(1)}, f32[192,128]{1,0:T(8,128)S(1)}, u32[]{:S(2)}, u32[]{:S(2)}) %collective-permute-start.5) | collective-permute-done | bytes 98336 | tf_op jit(solution)/shard_map/ppermute | solution.py:1033
  41.3 0.0 collective-permute-done.6.refs_2_
  41.3 0.0 collective-permute-done.7.refs_3_
  41.4 0.1 collective-permute-start.8
  41.4 1.4 %collective-permute-done.8.refs_1_ = f32[384,128]{1,0:T(8,128)S(1)} collective-permute-done((f32[384,128]{1,0:T(8,128)S(1)}, f32[384,128]{1,0:T(8,128)S(1)}, u32[]{:S(2)}, u32[]{:S(2)}) %collective-permute-start.8) | collective-permute-done | bytes 196640 | tf_op jit(solution)/shard_map/ppermute | solution.py:1033
  42.9 7.6 %shard_map.101 = (f32[20,12800]{1,0:T(8,128)}, f32[2,128]{1,0:T(2,128)}, f32[2608,128]{1,0:T(8,128)S(1)}, f32[2608,128]{1,0:T(8,128)S(1)}, f32[2608,128]{1,0:T(8...) custom-call(f32[384,128]{1,0:T(8,128)S(1)} %shard_map.100.refs_0_, ...), custom_call_target="tpu_custom_call", output_to_operand_aliasing={{2}: (4, {}), {3}: (5, {}), {4}: (6, {}), {5}: (7, {}), {6}... | custom-call | bytes 42000000 | tf_op jit(solution)/shard_map/pallas_call | solution.py:949
  (2 shorter events, 0.0 us)
Async XLA Ops:
  0.6 5.8 %copy-start = (f32[2,128]{1,0:T(2,128)S(1)}, f32[2,128]{1,0:T(2,128)}, u32[]{:S(2)}) copy-start(f32[2,128]{1,0:T(2,128)} %inverse.1) | copy-start | bytes 3076
  5.2 9.5 %collective-permute-start = (bf16[1200,128]{1,0:T(8,128)(2,1)}, bf16[1200,128]{1,0:T(8,128)(2,1)S(1)}, u32[]{:S(2)}, u32[]{:S(2)}) collective-permute-start(bf16[1200,128]{1,0:T(8,128)(2,1)} %get-tuple-element.27), channel_id=1, source_target_pairs={{0,1},{1,0},{2,3},{3,2},{4,5},{5,4},{6,7},{7,6},{8,9},{9,8},{10,11... | collective-permute-start | bytes 921608 | tf_op jit(solution)/shard_map/ppermute | solution.py:983
  5.7 8.9 %collective-permute-start.1 = (bf16[1200,128]{1,0:T(8,128)(2,1)}, bf16[1200,128]{1,0:T(8,128)(2,1)S(1)}, u32[]{:S(2)}, u32[]{:S(2)}) collective-permute-start(bf16[1200,128]{1,0:T(8,128)(2,1)} %get-tuple-element.28), channel_id=1, source_target_pairs={{1,2},{2,1},{3,4},{4,3},{5,6},{6,5},{7,8},{8,7},{9,10},{10,9},{11,... | collective-permute-start | bytes 921608 | tf_op jit(solution)/shard_map/ppermute | solution.py:985
  18.2 23.2 %collective-permute-start.6 = (bf16[1504,128]{1,0:T(8,128)(2,1)S(1)}, bf16[1504,128]{1,0:T(8,128)(2,1)S(1)}, u32[]{:S(2)}, u32[]{:S(2)}) collective-permute-start(bf16[1504,128]{1,0:T(8,128)(2,1)S(1)} %get-tuple-element.46), channel_id=1, source_target_pairs={{0,1},{1,0},{2,3},{3,2},{4,5},{5,4},{6,7},{7,6},{8,9},{9,8},{10,11... | collective-permute-start | bytes 1155080 | tf_op jit(solution)/shard_map/ppermute | solution.py:983
  22.1 19.2 %collective-permute-start.7 = (bf16[1504,128]{1,0:T(8,128)(2,1)S(1)}, bf16[1504,128]{1,0:T(8,128)(2,1)S(1)}, u32[]{:S(2)}, u32[]{:S(2)}) collective-permute-start(bf16[1504,128]{1,0:T(8,128)(2,1)S(1)} %get-tuple-element.47), channel_id=1, source_target_pairs={{1,2},{2,1},{3,4},{4,3},{5,6},{6,5},{7,8},{8,7},{9,10},{10,9},{11,... | collective-permute-start | bytes 1155080 | tf_op jit(solution)/shard_map/ppermute | solution.py:985
  25.7 9.8 %collective-permute-start.4 = (f32[48,128]{1,0:T(8,128)S(1)}, f32[48,128]{1,0:T(8,128)S(1)}, u32[]{:S(2)}, u32[]{:S(2)}) collective-permute-start(f32[48,128]{1,0:T(8,128)S(1)} %shard_map.98.refs_0_), channel_id=1, source_target_pairs={{0,12},{1,13},{2,14},{3,15},{4,8},{5,9},{6,10},{7,11},{8,4},{9,5},... | collective-permute-start | bytes 73736 | tf_op jit(solution)/shard_map/ppermute | solution.py:1033
  31.9 4.7 %collective-permute-start.3 = (f32[48,128]{1,0:T(8,128)S(1)}, f32[48,128]{1,0:T(8,128)S(1)}, u32[]{:S(2)}, u32[]{:S(2)}) collective-permute-start(f32[48,128]{1,0:T(8,128)S(1)} %shard_map.98.refs_0_), channel_id=1, source_target_pairs={{0,8},{1,9},{2,10},{3,11},{4,12},{5,13},{6,14},{7,15},{8,0},{9,1},... | collective-permute-start | bytes 73736 | tf_op jit(solution)/shard_map/ppermute | solution.py:1033
  31.9 4.7 %collective-permute-start.2 = (f32[48,128]{1,0:T(8,128)S(1)}, f32[48,128]{1,0:T(8,128)S(1)}, u32[]{:S(2)}, u32[]{:S(2)}) collective-permute-start(f32[48,128]{1,0:T(8,128)S(1)} %shard_map.98.refs_0_), channel_id=1, source_target_pairs={{0,4},{1,5},{2,6},{3,7},{4,0},{5,1},{6,2},{7,3},{8,12},{9,13},{10,... | collective-permute-start | bytes 73736 | tf_op jit(solution)/shard_map/ppermute | solution.py:1033
  36.6 4.7 %collective-permute-start.5 = (f32[192,128]{1,0:T(8,128)S(1)}, f32[192,128]{1,0:T(8,128)S(1)}, u32[]{:S(2)}, u32[]{:S(2)}) collective-permute-start(f32[192,128]{1,0:T(8,128)S(1)} %shard_map.99.refs_0_), channel_id=1, source_target_pairs={{0,2},{1,3},{2,0},{3,1},{4,6},{5,7},{6,4},{7,5},{8,10},{9,11},{10,... | collective-permute-start | bytes 294920 | tf_op jit(solution)/shard_map/ppermute | solution.py:1033
  41.4 1.5 %collective-permute-start.8 = (f32[384,128]{1,0:T(8,128)S(1)}, f32[384,128]{1,0:T(8,128)S(1)}, u32[]{:S(2)}, u32[]{:S(2)}) collective-permute-start(f32[384,128]{1,0:T(8,128)S(1)} %shard_map.100.refs_0_), channel_id=1, source_target_pairs={{0,1},{1,0},{2,3},{3,2},{4,5},{5,4},{6,7},{7,6},{8,9},{9,8},{10,11... | collective-permute-start | bytes 589832 | tf_op jit(solution)/shard_map/ppermute | solution.py:1033
